TPU v7x, 32 devices: a whole 2x2x4 slice. The times are simulated.
32 devices in a mesh: dp: 8 (over z, x), fsdp: 4 (over y, core).
Axes of the slice: x: 2, y: 2, z: 4, core: 2. Of those that a mesh axis runs over, the one named last changes fastest.
Arguments:
- tokens: bfloat16 [32768, 512], P(('dp', 'fsdp')), may hold values from -6 to 6
- cotangent: bfloat16 [32768, 512], P(('dp', 'fsdp')), may hold values from -6 to 6
- attention_params: bfloat16 [1048576], P(('dp', 'fsdp')), may hold values from -0.25 to 0.25
- feedforward_params: bfloat16 [2097152], P(('dp', 'fsdp')), may hold values from -0.25 to 0.25
- bias_params: bfloat16 [4096], P(('dp', 'fsdp')), may hold values from -3 to 3
- branch_gates: float32 [2], replicated, may hold values from 0.5 to 2
- bucket_counts: int32 [32, 3], P(('dp', 'fsdp')), may hold values from 0 to 8, as said below
- valid_lengths: int32 [32, 8], P(('dp', 'fsdp')), may hold values from 0 to 1024, as said below
Outputs:
- layer_output: bfloat16 [32768, 512], P(('dp', 'fsdp'))
- input_grad: float32 [32768, 512], P(('dp', 'fsdp'))
- attention_grad: float32 [1048576], P(('dp', 'fsdp'))
- feedforward_grad: float32 [2097152], P(('dp', 'fsdp'))
- bias_grad: float32 [4096], P(('dp', 'fsdp'))
- gate_grad: float32 [2], replicated
Inputs may be any that keep to these rules, and one draw needn't show every extreme that they name: `bucket_counts`: row r counts slots of 128, 512 and 1024 rows in that order; the slots fill exactly 1024 rows. `valid_lengths`: entry (r, s) lies between half the size of slot s of buffer r (rounded up) and that size, and is 0 for slots beyond the buffer's count.
All inputs are finite; a program needn't handle non-finite values.
Results may differ from a plain program's by a relative error of at most 0.012.
The roundings to bfloat16 on the way count: a program that leaves them out, or rounds other values in their place, can miss the bound.
Values may be sent and summed in bfloat16 or wider, within the bound.
No kernel may reach another device: no remote copies, remote signals or barrier semaphores. Data moves between devices by JAX's collectives and lax.ppermute only.
A program may use at most 128 MiB of HBM per device.

v0:
```python
from functools import partial
import math

import jax
import jax.numpy as jnp
from jax import lax
from jax.sharding import PartitionSpec as P

D = 512
H = 8
HD = 64
FF = 2048
TOK_DEV = 1024
SLOTS = 8
SHORT = 128
MID = 512
LONG = 1024


def project(former, latter):
    return jnp.dot(former, latter, preferred_element_type=jnp.float32)


def project_back(former, latter):
    return lax.dot_general(
        former, latter, (((1,), (1,)), ((), ())), preferred_element_type=jnp.float32
    )


def outer_sum(former, latter):
    return lax.dot_general(
        former, latter, (((0,), (0,)), ((), ())), preferred_element_type=jnp.float32
    )


def layout(slot_counts, lengths):
    slot_ids = jnp.arange(SLOTS)
    first_end = slot_counts[2]
    second_end = first_end + slot_counts[1]
    third_end = second_end + slot_counts[0]
    slot_sizes = jnp.where(
        slot_ids < first_end,
        LONG,
        jnp.where(slot_ids < second_end, MID, jnp.where(slot_ids < third_end, SHORT, 0)),
    ).astype(jnp.int32)
    slot_ends = jnp.cumsum(slot_sizes)
    slot_starts = slot_ends - slot_sizes
    finish = jnp.where(slot_sizes > 0, slot_ends, TOK_DEV)
    position = jnp.arange(TOK_DEV)
    member = (position[:, None] >= finish[None, :]).astype(jnp.int32)
    slot_of = jnp.sum(member, axis=1)
    chosen = (slot_of[:, None] == slot_ids[None, :]).astype(jnp.int32)
    offset = position - jnp.sum(chosen * slot_starts[None, :], axis=1)
    usable = offset < jnp.sum(chosen * lengths[None, :], axis=1)
    return (slot_of, usable)


def split_square(flat, count):
    block_size = D * D
    return [
        flat[index * block_size : (index + 1) * block_size].reshape(D, D) for index in range(count)
    ]


def block_scores(queries, key_rows, slot_block, slot_of, usable):
    scaling = 1.0 / math.sqrt(HD)
    raw_scores = (
        jnp.einsum("qhd,khd->hqk", queries, key_rows, preferred_element_type=jnp.float32) * scaling
    )
    allowed = (slot_block[:, None] == slot_of[None, :]) & usable[None, :]
    return jnp.where(allowed[None], raw_scores, -1e30)


def block_forward(key_rows, value_rows, slot_of, usable, pieces):
    queries, slot_block = pieces
    scores = block_scores(queries, key_rows, slot_block, slot_of, usable)
    largest = jnp.max(scores, axis=-1, keepdims=True)
    shifted = jnp.exp(scores - largest)
    total = jnp.sum(shifted, axis=-1, keepdims=True)
    probs = (shifted / total).astype(jnp.bfloat16)
    context = jnp.einsum("hqk,khd->qhd", probs, value_rows, preferred_element_type=jnp.float32)
    return (context, largest + jnp.log(total))


def block_backward(key_rows, value_rows, slot_of, usable, carry, pieces):
    scaling = 1.0 / math.sqrt(HD)
    grad_key, grad_value = carry
    queries, grad_context, slot_block, log_total = pieces
    scores = block_scores(queries, key_rows, slot_block, slot_of, usable)
    probs = jnp.exp(scores - log_total)
    grad_probs = jnp.einsum(
        "qhd,khd->hqk", grad_context, value_rows, preferred_element_type=jnp.float32
    )
    inner = jnp.sum(probs * grad_probs, axis=-1, keepdims=True)
    grad_scores = (probs * (grad_probs - inner)).astype(jnp.bfloat16)
    grad_query = (
        jnp.einsum("hqk,khd->qhd", grad_scores, key_rows, preferred_element_type=jnp.float32)
        * scaling
    )
    grad_key = (
        grad_key
        + jnp.einsum("hqk,qhd->khd", grad_scores, queries, preferred_element_type=jnp.float32)
        * scaling
    )
    grad_value = grad_value + jnp.einsum(
        "hqk,qhd->khd", probs.astype(jnp.bfloat16), grad_context, preferred_element_type=jnp.float32
    )
    return ((grad_key, grad_value), grad_query)


def spread_feedforward(flat):
    return lax.psum_scatter(flat, ("dp", "fsdp"), scatter_dimension=0, tiled=True)


def spread_attention(weight_flat, bias_flat):
    return (
        lax.psum_scatter(weight_flat, ("dp", "fsdp"), scatter_dimension=0, tiled=True),
        lax.psum_scatter(bias_flat, ("dp", "fsdp"), scatter_dimension=0, tiled=True),
    )


def local(
    tokens,
    cotangent,
    attention_params,
    feedforward_params,
    bias_params,
    branch_gates,
    bucket_counts,
    valid_lengths,
):
    slot_of, usable = layout(bucket_counts[0], valid_lengths[0])
    attention_all, bias_all = (
        lax.all_gather(attention_params, ("dp", "fsdp"), axis=0, tiled=True),
        lax.all_gather(bias_params, ("dp", "fsdp"), axis=0, tiled=True),
    )
    w_query, w_key, w_value, w_out = split_square(attention_all, 4)
    b_query = bias_all[0:D]
    b_value = bias_all[D : 2 * D]
    b_out = bias_all[2 * D : 3 * D]
    b_down = bias_all[3 * D : 4 * D]
    b_up = bias_all[4 * D :]
    gate_attend = branch_gates[0]
    gate_feed = branch_gates[1]
    queries = (project(tokens, w_query) + b_query).astype(jnp.bfloat16)
    key_rows = project(tokens, w_key).astype(jnp.bfloat16)
    value_rows = (project(tokens, w_value) + b_value).astype(jnp.bfloat16)
    block = min(512, TOK_DEV)
    count = TOK_DEV // block
    query_blocks = queries.reshape(count, block, H, HD)
    slot_blocks = slot_of.reshape(count, block)
    key_heads = key_rows.reshape(TOK_DEV, H, HD)
    value_heads = value_rows.reshape(TOK_DEV, H, HD)
    contexts, log_totals = lax.map(
        partial(block_forward, key_heads, value_heads, slot_of, usable), (query_blocks, slot_blocks)
    )
    context = contexts.reshape(TOK_DEV, D).astype(jnp.bfloat16)
    feedforward_all = lax.all_gather(feedforward_params, ("dp", "fsdp"), axis=0, tiled=True)
    w_up = feedforward_all[0 : D * FF].reshape(D, FF)
    w_down = feedforward_all[D * FF :].reshape(FF, D)
    branch = project(context, w_out) + b_out
    middle = tokens.astype(jnp.float32) + gate_attend * branch
    middle_low = middle.astype(jnp.bfloat16)
    hidden = project(middle_low, w_up) + b_up
    active = jax.nn.gelu(hidden).astype(jnp.bfloat16)
    second = project(active, w_down) + b_down
    layer_output = (middle + gate_feed * second).astype(jnp.bfloat16)
    feedforward_again = lax.all_gather(feedforward_params, ("dp", "fsdp"), axis=0, tiled=True)
    w_up_back = feedforward_again[0 : D * FF].reshape(D, FF)
    w_down_back = feedforward_again[D * FF :].reshape(FF, D)
    hidden_back = project(middle_low, w_up_back) + b_up
    grad_output = cotangent.astype(jnp.float32)
    gate_feed_grad = jnp.sum(second * grad_output)
    grad_second = (gate_feed * grad_output).astype(jnp.bfloat16)
    grad_w_down = outer_sum(active, grad_second)
    grad_b_down = jnp.sum(grad_second.astype(jnp.float32), axis=0)
    grad_active = project_back(grad_second, w_down_back)
    gelu_out, gelu_back = jax.vjp(jax.nn.gelu, hidden_back)
    grad_hidden = gelu_back(grad_active)[0].astype(jnp.bfloat16)
    grad_w_up = outer_sum(middle_low, grad_hidden)
    grad_b_up = jnp.sum(grad_hidden.astype(jnp.float32), axis=0)
    grad_middle = grad_output + project_back(grad_hidden, w_up_back)
    feedforward_grad = spread_feedforward(
        jnp.concatenate([grad_w_up.reshape(-1), grad_w_down.reshape(-1)])
    )
    attention_again = lax.all_gather(attention_params, ("dp", "fsdp"), axis=0, tiled=True)
    w_query_back, w_key_back, w_value_back, w_out_back = split_square(attention_again, 4)
    gate_attend_grad = jnp.sum(branch * grad_middle)
    grad_branch = (gate_attend * grad_middle).astype(jnp.bfloat16)
    grad_w_out = outer_sum(context, grad_branch)
    grad_b_out = jnp.sum(grad_branch.astype(jnp.float32), axis=0)
    grad_context = (
        project_back(grad_branch, w_out_back).astype(jnp.bfloat16).reshape(count, block, H, HD)
    )
    zero_heads = jnp.zeros((TOK_DEV, H, HD), jnp.float32)
    (grad_key, grad_value), grad_query_blocks = lax.scan(
        partial(block_backward, key_heads, value_heads, slot_of, usable),
        (zero_heads, zero_heads),
        (query_blocks, grad_context, slot_blocks, log_totals),
    )
    grad_query = grad_query_blocks.reshape(TOK_DEV, D).astype(jnp.bfloat16)
    grad_key = grad_key.reshape(TOK_DEV, D).astype(jnp.bfloat16)
    grad_value = grad_value.reshape(TOK_DEV, D).astype(jnp.bfloat16)
    grad_w_query = outer_sum(tokens, grad_query)
    grad_w_key = outer_sum(tokens, grad_key)
    grad_w_value = outer_sum(tokens, grad_value)
    input_grad = (
        grad_middle
        + project_back(grad_query, w_query_back)
        + project_back(grad_key, w_key_back)
        + project_back(grad_value, w_value_back)
    )
    grad_b_query = jnp.sum(grad_query.astype(jnp.float32), axis=0)
    grad_b_value = jnp.sum(grad_value.astype(jnp.float32), axis=0)
    attention_flat = jnp.concatenate(
        [
            grad_w_query.reshape(-1),
            grad_w_key.reshape(-1),
            grad_w_value.reshape(-1),
            grad_w_out.reshape(-1),
        ]
    )
    bias_flat = jnp.concatenate([grad_b_query, grad_b_value, grad_b_out, grad_b_down, grad_b_up])
    attention_grad, bias_grad = spread_attention(attention_flat, bias_flat)
    gate_grad = lax.psum(jnp.stack([gate_attend_grad, gate_feed_grad]), ("dp", "fsdp"))
    return (layer_output, input_grad, attention_grad, feedforward_grad, bias_grad, gate_grad)


def solution(mesh):
    in_specs = (
        P(("dp", "fsdp"), None),
        P(("dp", "fsdp"), None),
        P(("dp", "fsdp")),
        P(("dp", "fsdp")),
        P(("dp", "fsdp")),
        P(),
        P(("dp", "fsdp"), None),
        P(("dp", "fsdp"), None),
    )
    out_specs = (
        P(("dp", "fsdp"), None),
        P(("dp", "fsdp"), None),
        P(("dp", "fsdp")),
        P(("dp", "fsdp")),
        P(("dp", "fsdp")),
        P(),
    )
    return jax.shard_map(local, mesh=mesh, in_specs=in_specs, out_specs=out_specs, check_vma=False)
```

profile of v0, /device:TPU:0, one launch (start us, length us, event | category | flops | bytes accessed | tf_op | source)
XLA Modules:
  0.0 549.0 jit_solution(14944329254577472005)
XLA Ops:
  8.7 43.2 %all-gather = bf16[32,1,128]{2,1,0:T(2,128)(2,1)S(1)} all-gather(bf16[1,1,128]{2,1,0:T(2,128)(2,1)} %bitcast.201), channel_id=1, replica_groups=mesh['dp'=8,'fsdp'=4] {'dp','fsdp'}, dimensions={0}, use_global_device_ids=true | all-gather | bytes 8448 | tf_op jit(solution)/shard_map/all_gather | solution.py:135
  60.2 9.8 %all-gather.4.cloned.1.call-done = bf16[1048576]{0:T(1024)(128)(2,1)} async-done(((bf16[32768]{0:T(1024)(128)(2,1)}), bf16[1048576]{0:T(1024)(128)(2,1)}) %all-gather.4.cloned.1.call-update) | async-done | bytes 2097168 | tf_op jit(solution)/shard_map/all_gather | solution.py:134
  84.0 3.1 add_convert_fusion.1
  87.1 30.7 %while.27 = (s32[]{:T(128)}, bf16[2,512,8,64]{1,3,2,0:T(8,128)(2,1)S(1)}, f32[2,8,512,1]{2,1,3,0:T(8,128)}, s32[2,512]{1,0:T(2,128)S(1)}, s32[1024]{0:T(1024)S(1...) while((s32[]{:T(128)}, ...), condition=%wide.region_7.8_spmd, body=%wide.region_4.7_spmd.sunk | while | flops 1125117952 | bytes 56241276 | solution.py:154
  87.6 4.1 fusion.108
  91.7 4.2 fusion.109
  96.0 5.9 %fusion.110 = bf16[2,512,8,64]{1,3,2,0:T(8,128)(2,1)S(1)} fusion(bf16[2,512,8,64]{1,3,2,0:T(8,128)(2,1)S(1)} %get-tuple-element.481, s32[]{:T(128)S(6)} %copy.65, bf16[1024,8,64]{0,2,1:T(8,128)(2,1)} %get-tuple-element.498, f32[8,512,1024]{2,1,0:T(8,128)S(1)} %get-tuple-element.454, f32[8,512]{1,0:T(8,128)S(1)} %fusion.109, ...), kind=kOutput, calls=%fused_computation.8.clone.1 | convolution fusion | flops 557842432 | bytes 19431428 | tf_op jit(solution)/shard_map/while/body/eval_jaxpr/hqk,khd->qhd/dot_general | solution.py:81
  102.9 4.1 fusion.108
  107.1 4.2 fusion.109
  111.3 5.9 %fusion.110 = bf16[2,512,8,64]{1,3,2,0:T(8,128)(2,1)S(1)} fusion(bf16[2,512,8,64]{1,3,2,0:T(8,128)(2,1)S(1)} %get-tuple-element.481, s32[]{:T(128)S(6)} %copy.65, bf16[1024,8,64]{0,2,1:T(8,128)(2,1)} %get-tuple-element.498, f32[8,512,1024]{2,1,0:T(8,128)S(1)} %get-tuple-element.454, f32[8,512]{1,0:T(8,128)S(1)} %fusion.109, ...), kind=kOutput, calls=%fused_computation.8.clone.1 | convolution fusion | flops 557842432 | bytes 19431428 | tf_op jit(solution)/shard_map/while/body/eval_jaxpr/hqk,khd->qhd/dot_general | solution.py:81
  120.2 3.1 fusion.39
  123.3 10.5 %all-gather.6.cloned.1.call-done = bf16[2097152]{0:T(1024)(128)(2,1)} async-done(((bf16[65536]{0:T(1024)(128)(2,1)}), bf16[2097152]{0:T(1024)(128)(2,1)}) %all-gather.6.cloned.1.call-update) | async-done | bytes 4194320 | tf_op jit(solution)/shard_map/all_gather | solution.py:158
  133.8 3.8 fusion.42
  137.6 4.8 slice.137
  144.8 5.8 %multiply_convert_fusion.1 = (bf16[1024,2048]{1,0:T(8,128)(2,1)S(1)}, f32[1024,2048]{1,0:T(8,128)S(1)}) fusion(f32[2048]{0:T(1024)S(1)} %bitcast.196, bf16[1024,512]{1,0:T(8,128)(2,1)} %get-tuple-element.327, bf16[512,2048]{1,0:T(8,128)(2,1)} %slice.134), kind=kOutput, calls=%fused_computation.54 | convolution fusion | flops 2168455168 | bytes 15736832 | tf_op jit(solution)/shard_map/dot_general | solution.py:21
  156.0 9.0 %convert_reduce_fusion = (f32[2048]{0:T(1024)}, bf16[1024,2048]{1,0:T(8,128)(2,1)S(1)}) fusion(f32[1024,2048]{1,0:T(8,128)S(1)} %get-tuple-element.330, f32[2048]{0:T(1024)S(1)} %bitcast.197, bf16[2048,512]{1,0:T(8,128)(2,1)S(1)} %copy-done.18, bf16[1024,512]{1,0:T(8,128)(2,1)S(1)} %copy-done.32, f32[]{:T(128)} %bitcast.17), kind=kOutput, calls=%fused_computation.53 | convolution fusion | flops 2197288960 | bytes 15745028 | tf_op jit(solution)/shard_map/dot_general | solution.py:25
  167.5 7.2 %multiply_reduce_fusion.1 = (f32[]{:T(128)}, bf16[1024,512]{1,0:T(8,128)(2,1)}, f32[512]{0:T(512)}, f32[]{:T(128)}, f32[512]{0:T(512)}, /*index=5*/bf16[1024,512]{1,0:T(8,128)(2,1)S(1)}, f32[1024,512]{1,0:T(8,128)}) fusion(f32[1024,512]{1,0:T(8,128)S(1)} %copy-done.16, f32[512]{0:T(512)S(1)} %bitcast.195, f32[1024,512]{1,0:T(8,128)S(1)} %fusion.46, ...), kind=kOutput, calls=%fused_computation.63 | convolution fusion | flops 2159016960 | bytes 16785424 | tf_op jit(solution)/shard_map/dot_general | solution.py:25
  178.4 3.0 copy.58
  190.4 87.9 %while.28 = (s32[]{:T(128)}, f32[1024,8,64]{0,2,1:T(8,128)}, f32[1024,8,64]{0,2,1:T(8,128)}, bf16[2,512,8,64]{1,3,2,0:T(8,128)(2,1)}, bf16[2,512,8,64]{1,3,2,0:T...) while((s32[]{:T(128)}, f32[1024,8,64]{0,2,1:T(8,128)}, ...), condition=%wide.region_10.11_spmd.clone, body=%wide.region_8.10_spmd.clone.sunk | while | flops 2726031360 | bytes 187788576 | solution.py:196
  193.2 3.8 fusion.120
  196.9 11.4 %multiply_reduce_fusion.3 = (f32[8,512]{1,0:T(8,128)}, f32[8,512,1024]{2,1,0:T(8,128)}) fusion(f32[8,512,1024]{2,1,0:T(8,128)S(1)} %fusion.120, f32[8,512]{1,0:T(8,128)} %dynamic-slice_bitcast_fusion.2, bf16[1024,8,64]{0,2,1:T(8,128)(2,1)S(1)} %get-tuple-element.536, bf16[2,512,8,64]{1,3,2,0:T(8,128)(2,1)} %get-tuple-element.532, s32[]{:T(128)S(6)} %copy.75, ...), kind=kOutput, calls=%fused_computation.18.clone.1 | convolution fusion | flops 557838336 | bytes 35684356 | tf_op jit(solution)/shard_map/while/body/eval_jaxpr/qhd,khd->hqk/dot_general | solution.py:68
  208.4 9.4 %multiply_convert_fusion.5 = bf16[8,512,1024]{2,1,0:T(8,128)(2,1)} fusion(f32[8,512,1024]{2,1,0:T(8,128)} %get-tuple-element.468, f32[8,512,1024]{2,1,0:T(8,128)S(1)} %fusion.120, f32[8,512]{1,0:T(8,128)} %get-tuple-element.469), kind=kLoop, calls=%fused_computation.17.clone.1 | loop fusion | flops 12582912 | bytes 41959424 | tf_op jit(solution)/shard_map/while/body/eval_jaxpr/convert_element_type | solution.py:95
  217.7 8.9 %bitcast_add_fusion.5 = f32[1024,8,64]{0,2,1:T(8,128)} fusion(f32[1024,8,64]{0,2,1:T(8,128)} %get-tuple-element.516, f32[8,512,1024]{2,1,0:T(8,128)} %get-tuple-element.468, pred[]{:T(512)S(6)} %compare.3, bf16[2,512,8,64]{1,3,2,0:T(8,128)(2,1)S(1)} %copy-done.1, s32[]{:T(128)S(6)} %copy.75), kind=kOutput, calls=%fused_computation.22.clone.1 | convolution fusion | flops 542113792 | bytes 21495812 | tf_op jit(solution)/shard_map/while/body/eval_jaxpr/hqk,qhd->khd/dot_general | solution.py:105
  229.3 4.4 bitcast_add_fusion.4
  236.2 3.8 fusion.120
  240.0 11.4 %multiply_reduce_fusion.3 = (f32[8,512]{1,0:T(8,128)}, f32[8,512,1024]{2,1,0:T(8,128)}) fusion(f32[8,512,1024]{2,1,0:T(8,128)S(1)} %fusion.120, f32[8,512]{1,0:T(8,128)} %dynamic-slice_bitcast_fusion.2, bf16[1024,8,64]{0,2,1:T(8,128)(2,1)S(1)} %get-tuple-element.536, bf16[2,512,8,64]{1,3,2,0:T(8,128)(2,1)} %get-tuple-element.532, s32[]{:T(128)S(6)} %copy.75, ...), kind=kOutput, calls=%fused_computation.18.clone.1 | convolution fusion | flops 557838336 | bytes 35684356 | tf_op jit(solution)/shard_map/while/body/eval_jaxpr/qhd,khd->hqk/dot_general | solution.py:68
  251.4 9.4 %multiply_convert_fusion.5 = bf16[8,512,1024]{2,1,0:T(8,128)(2,1)} fusion(f32[8,512,1024]{2,1,0:T(8,128)} %get-tuple-element.468, f32[8,512,1024]{2,1,0:T(8,128)S(1)} %fusion.120, f32[8,512]{1,0:T(8,128)} %get-tuple-element.469), kind=kLoop, calls=%fused_computation.17.clone.1 | loop fusion | flops 12582912 | bytes 41959424 | tf_op jit(solution)/shard_map/while/body/eval_jaxpr/convert_element_type | solution.py:95
  260.8 9.5 %bitcast_add_fusion.5 = f32[1024,8,64]{0,2,1:T(8,128)} fusion(f32[1024,8,64]{0,2,1:T(8,128)} %get-tuple-element.516, f32[8,512,1024]{2,1,0:T(8,128)} %get-tuple-element.468, pred[]{:T(512)S(6)} %compare.3, bf16[2,512,8,64]{1,3,2,0:T(8,128)(2,1)S(1)} %copy-done.1, s32[]{:T(128)S(6)} %copy.75), kind=kOutput, calls=%fused_computation.22.clone.1 | convolution fusion | flops 542113792 | bytes 21495812 | tf_op jit(solution)/shard_map/while/body/eval_jaxpr/hqk,qhd->khd/dot_general | solution.py:105
  273.0 5.1 bitcast_add_fusion.4
  299.3 6.5 %pad_maximum_fusion = f32[2097152]{0:T(1024)} fusion(f32[1048576]{0:T(1024)} %bitcast.173, f32[1048576]{0:T(1024)} %bitcast.174), kind=kLoop, calls=%fused_computation.52 | loop fusion | flops 2097152 | bytes 16777216 | tf_op jit(solution)/shard_map/concatenate | solution.py:184
  311.2 41.0 %all-reduce.3 = (f32[4096]{0:T(1024)S(1)}, f32[2]{0:T(128)}) all-reduce(f32[4096]{0:T(1024)S(1)} %constant_dynamic-update-slice_fusion, f32[2]{0:T(128)S(1)} %pad_maximum_fusion.2), channel_id=4, replica_groups=mesh['dp'=8,'fsdp'=4] {'dp','fsdp'}, use_global_device_ids=true, to_apply=%region_18.19.clone | all-reduce | flops 4098 | bytes 32784
  358.9 180.1 %all-reduce.7.cloned.1.call-done = (f32[1048576]{0:T(1024)}, f32[2097152]{0:T(1024)}) async-done(((f32[1048576]{0:T(1024)}, f32[2097152]{0:T(1024)}), (f32[1048576]{0:T(1024)}, f32[2097152]{0:T(1024)})) %all-reduce.7.cloned.1.call-update) | async-done | bytes 12582928
  (161 shorter events, 95.5 us)
Async XLA Ops:
  7.2 62.8 %all-gather.4.cloned.1.call-start = ((), (), s32[]{:S(2)}) async-start(), calls=%async_computation | async-start | bytes 2162688 | tf_op jit(solution)/shard_map/all_gather | solution.py:134
  7.9 125.9 %all-gather.6.cloned.1.call-start = ((), (), s32[]{:S(2)}) async-start(), calls=%async_computation.1 | async-start | bytes 4325376 | tf_op jit(solution)/shard_map/all_gather | solution.py:158
  8.6 530.3 %all-reduce.7.cloned.1.call-start = ((), (), s32[]{:S(2)}) async-start(), calls=%async_computation.2 | async-start | bytes 25165824
  79.6 4.4 copy-start.31
  137.6 7.1 %copy-start.27 = (f32[16,1,128]{2,1,0:T(1,128)S(1)}, f32[16,1,128]{2,1,0:T(1,128)}, u32[]{:S(2)}) copy-start(f32[16,1,128]{2,1,0:T(1,128)} %slice_convert_fusion) | copy-start | bytes 24580
  144.7 5.8 %copy-start.18 = (bf16[2048,512]{1,0:T(8,128)(2,1)S(1)}, bf16[2048,512]{1,0:T(8,128)(2,1)}, u32[]{:S(2)}) copy-start(bf16[2048,512]{1,0:T(8,128)(2,1)} %slice.137) | copy-start | bytes 6291460
  156.0 9.0 %copy-start.5 = (bf16[1024,512]{1,0:T(8,128)(2,1)S(1)}, bf16[1024,512]{1,0:T(8,128)(2,1)}, u32[]{:S(2)}) copy-start(bf16[1024,512]{1,0:T(8,128)(2,1)} %get-tuple-element.327) | copy-start | bytes 3145732
  165.0 2.4 copy-start.16
  165.0 2.4 copy-start.17
  165.0 2.5 copy-start.22
  165.0 2.5 copy-start.30
  167.5 7.2 %copy-start.9 = (bf16[64,8,2,512]{3,1,2,0:T(8,128)(2,1)S(1)}, bf16[64,8,2,512]{3,1,2,0:T(8,128)(2,1)}, u32[]{:S(2)}) copy-start(bf16[64,8,2,512]{3,1,2,0:T(8,128)(2,1)} %copy-done.8) | copy-start | bytes 3145732
  167.5 7.9 %copy-start.20 = (bf16[512,512]{1,0:T(8,128)(2,1)S(1)}, bf16[512,512]{1,0:T(8,128)(2,1)}, u32[]{:S(2)}) copy-start(bf16[512,512]{1,0:T(8,128)(2,1)} %slice.130) | copy-start | bytes 1572868
  208.3 9.4 %copy-start.1 = (bf16[2,512,8,64]{1,3,2,0:T(8,128)(2,1)S(1)}, bf16[2,512,8,64]{1,3,2,0:T(8,128)(2,1)}, u32[]{:S(2)}) copy-start(bf16[2,512,8,64]{1,3,2,0:T(8,128)(2,1)} %get-tuple-element.538) | copy-start | bytes 3145732 | tf_op jit(solution)/shard_map/while
  217.7 8.9 %copy-start = (bf16[8,512,1024]{2,1,0:T(8,128)(2,1)S(1)}, bf16[8,512,1024]{2,1,0:T(8,128)(2,1)}, u32[]{:S(2)}) copy-start(bf16[8,512,1024]{2,1,0:T(8,128)(2,1)} %multiply_convert_fusion.5) | copy-start | bytes 25165828 | tf_op jit(solution)/shard_map/while
  217.7 8.9 %copy-start.2 = (bf16[2,512,8,64]{1,3,2,0:T(8,128)(2,1)S(1)}, bf16[2,512,8,64]{1,3,2,0:T(8,128)(2,1)}, u32[]{:S(2)}) copy-start(bf16[2,512,8,64]{1,3,2,0:T(8,128)(2,1)} %get-tuple-element.517) | copy-start | bytes 3145732 | tf_op jit(solution)/shard_map/while
  229.3 4.4 copy-start.3
  251.4 9.4 %copy-start.1 = (bf16[2,512,8,64]{1,3,2,0:T(8,128)(2,1)S(1)}, bf16[2,512,8,64]{1,3,2,0:T(8,128)(2,1)}, u32[]{:S(2)}) copy-start(bf16[2,512,8,64]{1,3,2,0:T(8,128)(2,1)} %get-tuple-element.538) | copy-start | bytes 3145732 | tf_op jit(solution)/shard_map/while
  260.8 9.5 %copy-start = (bf16[8,512,1024]{2,1,0:T(8,128)(2,1)S(1)}, bf16[8,512,1024]{2,1,0:T(8,128)(2,1)}, u32[]{:S(2)}) copy-start(bf16[8,512,1024]{2,1,0:T(8,128)(2,1)} %multiply_convert_fusion.5) | copy-start | bytes 25165828 | tf_op jit(solution)/shard_map/while
  260.8 9.5 %copy-start.2 = (bf16[2,512,8,64]{1,3,2,0:T(8,128)(2,1)S(1)}, bf16[2,512,8,64]{1,3,2,0:T(8,128)(2,1)}, u32[]{:S(2)}) copy-start(bf16[2,512,8,64]{1,3,2,0:T(8,128)(2,1)} %get-tuple-element.517) | copy-start | bytes 3145732 | tf_op jit(solution)/shard_map/while
  273.0 5.1 copy-start.3
  278.3 4.4 copy-start.23
  291.8 4.1 copy-start.24
  299.3 6.6 %copy-start.10 = (f32[64,4,8,128]{3,1,2,0:T(4,128)S(1)}, f32[64,4,8,128]{3,1,2,0:T(4,128)}, u32[]{:S(2)}) copy-start(f32[64,4,8,128]{3,1,2,0:T(4,128)} %copy.56) | copy-start | bytes 3145732
  299.3 6.6 %copy-start.11 = (f32[64,4,8,128]{3,1,2,0:T(4,128)S(1)}, f32[64,4,8,128]{3,1,2,0:T(4,128)}, u32[]{:S(2)}) copy-start(f32[64,4,8,128]{3,1,2,0:T(4,128)} %copy.53) | copy-start | bytes 3145732
  299.3 6.6 %copy-start.12 = (f32[64,4,8,128]{3,1,2,0:T(4,128)S(1)}, f32[64,4,8,128]{3,1,2,0:T(4,128)}, u32[]{:S(2)}) copy-start(f32[64,4,8,128]{3,1,2,0:T(4,128)} %copy.54) | copy-start | bytes 3145732
  308.1 3.0 copy-start.29
  308.1 3.0 copy-start.28
  308.1 3.1 copy-start.26
  309.6 47.2 %copy-start.7 = (bf16[1024,8,64]{0,2,1:T(8,128)(2,1)S(1)}, bf16[1024,8,64]{0,2,1:T(8,128)(2,1)}, u32[]{:S(2)}) copy-start(bf16[1024,8,64]{0,2,1:T(8,128)(2,1)} %copy-done.6) | copy-start | bytes 3145732
  352.2 4.5 copy-start.13
  352.2 4.5 copy-start.14
  (8 other events, 13.4 us)
Sparse Core Ops, SparseCore 0:
  10.9 59.0 all-gather.3
  72.9 60.8 all-gather.5
  308.3 230.6 all-reduce.6
where the time goes:
time: 553 us; the launch traced here: 549 us
  waiting for transfers between devices  202 us (37%)
  matrix products  138 us (25%)
  blocking collectives  84.2 us (15%)
  local copies, waits for them, and re-layouts  58.3 us (11%)
  other arithmetic  49.3 us (9%)
  between operations  16.4 us (3%)
    unnamed x4, waiting for transfers between devices  181 us
    all_gather x1, blocking collectives, local(): lax.all_gather(bias_params, ('dp', 'fsdp'), axis=0, tiled=True)  43.2 us
    unnamed x1, blocking collectives  41 us
    dot_general x4, matrix products, block_scores(): jnp.einsum('qhd,khd->hqk', queries, key_rows, preferred_element_type=jnp....  31.1 us
    dot_general x6, matrix products, project_back(): lax.dot_general(former, latter, (((1,), (1,)), ((), ())), preferred_eleme...  23.9 us
    unnamed x74, local copies, waits for them, and re-layouts  20.6 us
    convert_element_type x2, other arithmetic, block_backward(): grad_scores = (probs * (grad_probs - inner)).astype(jnp.bfloat16)  18.8 us
    dot_general x2, matrix products, block_backward(): jnp.einsum('hqk,qhd->khd', probs.astype(jnp.bfloat16), grad_context, pref...  18.4 us
  transfers between devices with their start and end apart: 3, of which 3 were waited for; matrix products, arithmetic and copies ran while one was open for 12% of the time, Pallas kernels for 0%

commit v1 on v0

v1 whole, which is shorter than its diff:
```python
from functools import partial

import jax
import jax.numpy as jnp
from jax import lax
from jax.experimental import pallas as pl
from jax.experimental.pallas import tpu as pltpu
from jax.sharding import PartitionSpec as P

D = 512
H = 8
HD = 64
FF = 2048
ROWS = 1024
SLOTS = 8
SHORT = 128
MID = 512
LONG = 1024
AXES = ("dp", "fsdp")
PARTS = 32
BF = jnp.bfloat16
F32 = jnp.float32
VMEM = pl.BlockSpec(memory_space=pltpu.VMEM)
SMEM = pl.BlockSpec(memory_space=pltpu.SMEM)


def nn(a, b):
    return lax.dot_general(a, b, (((1,), (0,)), ((), ())), preferred_element_type=F32)


def nt(a, b):
    return lax.dot_general(a, b, (((1,), (1,)), ((), ())), preferred_element_type=F32)


def tn(a, b):
    return lax.dot_general(a, b, (((0,), (0,)), ((), ())), preferred_element_type=F32)


def call(body, outs, ins, scratch, flops, moved, limit):
    return pl.pallas_call(
        body,
        out_shape=[jax.ShapeDtypeStruct(s, d) for s, d in outs],
        in_specs=ins,
        out_specs=[VMEM] * len(outs),
        scratch_shapes=[pltpu.VMEM(s, d) for s, d in scratch],
        compiler_params=pltpu.CompilerParams(vmem_limit_bytes=limit << 20),
        cost_estimate=pl.CostEstimate(flops=flops, bytes_accessed=moved, transcendentals=0),
    )


def slot_masks(counts, lengths, keys_out, rows_out):
    lane = lax.broadcasted_iota(jnp.int32, (1, 128), 1)
    slot = lane & 63
    longs, mids, shorts = counts[0, 2], counts[0, 1], counts[0, 0]
    in_long = jnp.minimum(slot, longs)
    in_mid = jnp.clip(slot - longs, 0, mids)
    in_short = jnp.clip(slot - longs - mids, 0, shorts)
    start = in_long * LONG + in_mid * MID + in_short * SHORT
    size = jnp.where(
        slot < longs,
        LONG,
        jnp.where(slot < longs + mids, MID, jnp.where(slot < longs + mids + shorts, SHORT, 0)),
    )
    valid = jnp.zeros((1, 128), jnp.int32)
    for s in range(SLOTS):
        valid = jnp.where(slot == s, lengths[0, s], valid)
    row = lax.broadcasted_iota(jnp.int32, (ROWS, 128), 0)
    member = (row >= start) & (row < start + size)
    usable = (row >= start) & (row < start + valid)
    for parity in range(2):
        here = (slot < SLOTS) & ((lane >= 64) if parity == 0 else (lane < 64))
        rows_out[parity] = jnp.where(here & member, 1.0, 0.0).astype(BF)
        keys_out[parity] = jnp.where(here & jnp.logical_not(usable), -1e30, 0.0).astype(BF)


def half_of(parity, shape):
    lane = lax.broadcasted_iota(jnp.int32, shape, len(shape) - 1)
    return (lane < 64) if parity == 0 else (lane >= 64)


def attend_body(
    n, counts, lengths, place, tok, gathered, q_out, k_out, v_out, ctx_out, lse_out, branch_out,
    w_out, bias_out, keys_mask, rows_mask, lse_cols,
):
    rows_each = D * 4 // n
    tiles = rows_each // 16

    def assemble(o, _):
        piece = o ^ place[0]
        square, row = o // (n // 4), (o % (n // 4)) * rows_each
        for i in range(tiles):
            for j in range(4):
                w_out[square, pl.ds(pl.multiple_of(row + 16 * i, 16), 16), 128 * j : 128 * j + 128] = (
                    gathered[piece, 4 * i + j]
                )
        tail = gathered[piece, 4 * tiles].astype(F32)
        bias_out[0:1, pl.ds(pl.multiple_of(o * 128, 128), 128)] = tail[0:1]
        return 0

    lax.fori_loop(0, n, assemble, 0)
    slot_masks(counts, lengths, keys_mask, rows_mask)

    def project(r, _):
        at = pl.ds(pl.multiple_of(r * 256, 256), 256)
        x = tok[at, :]
        q = (nn(x, w_out[0]) + bias_out[0:1, 0:D]).astype(BF)
        q_out[at, :] = (q.astype(F32) * 0.125).astype(BF)
        k_out[at, :] = nn(x, w_out[1]).astype(BF)
        v_out[at, :] = (nn(x, w_out[2]) + bias_out[0:1, D : 2 * D]).astype(BF)
        return 0

    lax.fori_loop(0, 4, project, 0)
    lse_cols[...] = jnp.zeros_like(lse_cols)

    def pair(p, _):
        lanes = pl.ds(pl.multiple_of(p * 128, 128), 128)
        kp = k_out[:, lanes]
        vp = v_out[:, lanes]
        keys, values = [], []
        for parity in range(2):
            mine = half_of(parity, (ROWS, 128))
            keys.append(jnp.where(mine, kp, keys_mask[parity]))
            values.append(jnp.where(mine, vp, jnp.zeros_like(vp)))
        for r in range(4):
            at = slice(r * 256, r * 256 + 256)
            qp = q_out[at, lanes]
            total = None
            lane = lax.broadcasted_iota(jnp.int32, (256, 128), 1)
            logs = lse_cols[at, :]
            for parity in range(2):
                qa = jnp.where(half_of(parity, (256, 128)), qp, rows_mask[parity, at])
                s = nt(qa, keys[parity])
                top = jnp.max(s, axis=1, keepdims=True)
                e = jnp.exp(s - top)
                mass = jnp.sum(e, axis=1, keepdims=True)
                probs = (e * (1.0 / mass)).astype(BF)
                part = nn(probs, values[parity])
                total = part if total is None else total + part
                logs = jnp.where(lane == 2 * p + parity, top + jnp.log(mass), logs)
            ctx_out[at, lanes] = total.astype(BF)
            lse_cols[at, :] = logs
        return 0

    lax.fori_loop(0, 4, pair, 0)
    lse_out[...] = lse_cols[...].T[0:8]

    def out(r, _):
        at = pl.ds(pl.multiple_of(r * 256, 256), 256)
        branch_out[at, :] = nn(ctx_out[at, :], w_out[3]) + bias_out[0:1, 2 * D : 3 * D]
        return 0

    lax.fori_loop(0, 4, out, 0)


def feed_body(
    n, place, gates, tok, branch, cot, ctx, w_out, bias, gathered,
    layer_out, gm_out, gctx_out, keep_out, send_out, wo_out, sums_out, gate_out,
    w1, w2, mlow, gbr, gs_all, active_all, gh_all,
):
    rows_up = D // (n // 2)
    rows_down = FF // (n // 2)
    tiles = rows_down // 16 * 4

    def assemble_up(o, _):
        piece = o ^ place[0]
        for i in range(rows_up // 16):
            for j in range(16):
                w1[pl.ds(pl.multiple_of(o * rows_up + 16 * i, 16), 16), 128 * j : 128 * j + 128] = (
                    gathered[piece, 16 * i + j]
                )
        return 0

    def assemble_down(o, _):
        piece = (o + n // 2) ^ place[0]
        for i in range(rows_down // 16):
            for j in range(4):
                w2[pl.ds(pl.multiple_of(o * rows_down + 16 * i, 16), 16), 128 * j : 128 * j + 128] = (
                    gathered[piece, 4 * i + j]
                )
        return 0

    lax.fori_loop(0, n // 2, assemble_up, 0)
    lax.fori_loop(0, n // 2, assemble_down, 0)
    ga, gf = gates[0], gates[1]
    sums_out[...] = jnp.zeros_like(sums_out)
    c1 = 0.7978845608028654
    c2 = 0.044715

    def rows(r, carry):
        attend_sum, feed_sum = carry
        at = pl.ds(pl.multiple_of(r * 256, 256), 256)
        br = branch[at, :]
        middle = tok[at, :].astype(F32) + ga * br
        low = middle.astype(BF)
        mlow[at, :] = low
        ct = cot[at, :].astype(F32)
        gs = (gf * ct).astype(BF)
        gs_all[at, :] = gs
        second = jnp.zeros((256, D), F32) + bias[0:1, 3 * D : 4 * D]
        gmid = ct
        for j in range(4):
            cols = slice(512 * j, 512 * j + 512)
            v = nn(low, w1[:, cols]) + bias[0:1, 4 * D + 512 * j : 4 * D + 512 * j + 512]
            back = nt(gs, w2[cols, :])
            v2 = v * v
            t = jnp.tanh(c1 * v * (1.0 + c2 * v2))
            half = 0.5 * (1.0 + t)
            active = (v * half).astype(BF)
            slope = half + (0.5 * c1) * v * (1.0 - t * t) * (1.0 + (3.0 * c2) * v2)
            gh = (slope * back).astype(BF)
            active_all[at, cols] = active
            gh_all[at, cols] = gh
            sums_out[0:1, 4 * D + 512 * j : 4 * D + 512 * j + 512] += jnp.sum(
                gh.astype(F32), axis=0, keepdims=True
            )
            second = second + nn(active, w2[cols, :])
            gmid = gmid + nt(gh, w1[:, cols])
        layer_out[at, :] = (middle + gf * second).astype(BF)
        gm_out[at, :] = gmid
        gb = (ga * gmid).astype(BF)
        gbr[at, :] = gb
        gctx_out[at, :] = nt(gb, w_out[3]).astype(BF)
        sums_out[0:1, 2 * D : 3 * D] += jnp.sum(gb.astype(F32), axis=0, keepdims=True)
        sums_out[0:1, 3 * D : 4 * D] += jnp.sum(gs.astype(F32), axis=0, keepdims=True)
        attend_sum = attend_sum + jnp.sum(br * gmid, axis=0, keepdims=True)
        feed_sum = feed_sum + jnp.sum(second * ct, axis=0, keepdims=True)
        return attend_sum, feed_sum

    zero = jnp.zeros((1, D), F32)
    attend_sum, feed_sum = lax.fori_loop(0, 4, rows, (zero, zero))
    gate_out[0:1, :] = attend_sum
    gate_out[1:2, :] = feed_sum
    wo_out[...] = tn(ctx[...], gbr[...])
    odd = place[1] == 1

    def store(even_owner, tile, even, other):
        keep_out[even_owner // 2, tile] = jnp.where(odd, other, even)
        send_out[even_owner // 2, tile] = jnp.where(odd, even, other).astype(send_out.dtype)

    for j in range(4):
        val = tn(mlow[...], gh_all[:, 512 * j : 512 * j + 512])
        for o in range(0, n // 2, 2):
            for i in range(rows_up // 16):
                for jj in range(4):
                    col = slice(128 * jj, 128 * jj + 128)
                    top = o * rows_up + 16 * i
                    store(o, 16 * i + 4 * j + jj, val[top : top + 16, col], val[top + rows_up : top + rows_up + 16, col])
    for j in range(4):
        val = tn(active_all[:, 512 * j : 512 * j + 512], gs_all[...])
        per = 512 // rows_down
        for o in range(0, per, 2):
            for i in range(rows_down // 16):
                for jj in range(4):
                    col = slice(128 * jj, 128 * jj + 128)
                    top = o * rows_down + 16 * i
                    store(
                        n // 2 + j * per + o, 4 * i + jj,
                        val[top : top + 16, col], val[top + rows_down : top + rows_down + 16, col],
                    )


def back_body(
    n, counts, lengths, place, tok, q_in, k_in, v_in, gctx, lse, wo_grad, sums, gate,
    dq_out, dk_out, dv_out, keep_out, send_out, keys_mask, rows_mask, k_t, dq_t, dk_acc, dv_acc, sum_row,
):
    rows_each = D * 4 // n
    tiles = rows_each // 16
    slot_masks(counts, lengths, keys_mask, rows_mask)
    k_t[...] = k_in[...].T

    def pair(p, _):
        lanes = pl.ds(pl.multiple_of(p * 128, 128), 128)
        kp = k_in[:, lanes]
        vp = v_in[:, lanes]
        dk_acc[...] = jnp.zeros_like(dk_acc)
        dv_acc[...] = jnp.zeros_like(dv_acc)
        for parity in range(2):
            mine = half_of(parity, (ROWS, 128))
            ka = jnp.where(mine, kp, keys_mask[parity])
            kt = k_t[pl.ds(pl.multiple_of(p * 128 + 64 * parity, 64), 64), :]
            logs = lse[pl.ds(2 * p + parity, 1), :]
            few = half_of(parity, (256, 128))
            for r in range(4):
                at = slice(r * 256, r * 256 + 256)
                qp = q_in[at, lanes]
                gp = gctx[at, lanes]
                none = jnp.zeros_like(qp)
                st = nt(ka, jnp.where(few, qp, rows_mask[parity, at]))
                pt = jnp.exp(st - logs[:, at])
                gp = jnp.where(few, gp, none)
                dpt = nt(vp, gp)
                delta = jnp.sum(pt * dpt, axis=0, keepdims=True)
                dst = (pt * (dpt - delta)).astype(BF)
                dk_acc[...] += nn(dst, jnp.where(few, qp, none))
                dv_acc[...] += nn(pt.astype(BF), gp)
                dq_t[pl.ds(pl.multiple_of(p * 128 + 64 * parity, 64), 64), at] = nn(kt, dst) * 0.125
        dk_out[:, lanes] = dk_acc[...].astype(BF)
        dv_out[:, lanes] = dv_acc[...].astype(BF)
        return 0

    lax.fori_loop(0, 4, pair, 0)
    dq_out[...] = dq_t[...].T.astype(BF)
    odd = place[1] == 1
    x_t = tok[...].T
    per = n // 4
    for square in range(4):
        if square == 3:
            val = wo_grad[...]
        else:
            val = nn(x_t, (dq_out, dk_out, dv_out)[square][...])
        for o in range(0, per, 2):
            for i in range(tiles):
                for j in range(4):
                    col = slice(128 * j, 128 * j + 128)
                    top = o * rows_each + 16 * i
                    even, other = val[top : top + 16, col], val[top + rows_each : top + rows_each + 16, col]
                    at = (square * per + o) // 2
                    keep_out[at, 4 * i + j] = jnp.where(odd, other, even)
                    send_out[at, 4 * i + j] = jnp.where(odd, even, other).astype(send_out.dtype)
    sum_row[...] = sums[...]
    sum_row[0:1, 0:D] = jnp.sum(dq_out[...].astype(F32), axis=0, keepdims=True)
    sum_row[0:1, D : 2 * D] = jnp.sum(dv_out[...].astype(F32), axis=0, keepdims=True)
    lane = lax.broadcasted_iota(jnp.int32, (1, 128), 1)
    gates = jnp.zeros((1, 128), F32)
    for g in range(2):
        gates = jnp.where(lane == 2 * place[2] + g, jnp.sum(gate[g : g + 1, :]), gates)
    high = gates.astype(BF).astype(F32)
    rest = gates - high
    mid = rest.astype(BF).astype(F32)
    low = rest - mid
    row = lax.broadcasted_iota(jnp.int32, (16, 128), 0)
    base = jnp.where(row == 1, high, jnp.where(row == 2, mid, jnp.where(row == 3, low, 0.0)))
    for o in range(0, n, 2):
        even = jnp.where(row == 0, sum_row[0:1, 128 * o : 128 * o + 128], base)
        other = jnp.where(row == 0, sum_row[0:1, 128 * o + 128 : 128 * o + 256], base)
        keep_out[o // 2, 4 * tiles] = jnp.where(odd, other, even)
        send_out[o // 2, 4 * tiles] = jnp.where(odd, even, other).astype(send_out.dtype)


def input_body(gm, dq, dk, dv, w, out):
    def rows(r, _):
        at = pl.ds(pl.multiple_of(r * 256, 256), 256)
        out[at, :] = gm[at, :] + nt(dq[at, :], w[0]) + nt(dk[at, :], w[1]) + nt(dv[at, :], w[2])
        return 0

    lax.fori_loop(0, 4, rows, 0)


def to_tiles(flat, rows, cols):
    return flat.reshape(rows // 16, 16, cols // 128, 128).transpose(0, 2, 1, 3).reshape(-1, 16, 128)


def from_tiles(tiles, rows, cols):
    return tiles.reshape(rows // 16, cols // 128, 16, 128).transpose(0, 2, 1, 3).reshape(-1)


def swap(x, n, bit):
    return lax.ppermute(x, AXES, [(i, i ^ bit) for i in range(n)])


def scatter(keep, send, me, n):
    got = swap(send, n, 1)
    total = keep + got.astype(F32)
    z, x, y = me // 8, (me // 4) % 2, (me // 2) % 2
    total = total.reshape((4, 2, 2) + keep.shape[1:])
    half = keep.shape[1] // 2

    def pick(v, axis, index):
        return lax.dynamic_index_in_dim(v, index, axis, keepdims=False)

    a, b = total[:, :, :, :half], total[:, :, :, half:]
    a_got = swap(pick(a, 1, 1 - x).astype(BF), n, 4)
    b_got = swap(pick(b, 2, 1 - y).astype(BF), n, 2)
    a = pick(a, 1, x) + a_got.astype(F32)
    b = pick(b, 2, y) + b_got.astype(F32)
    a_got = swap(pick(a, 1, 1 - y).astype(BF), n, 2)
    b_got = swap(pick(b, 1, 1 - x).astype(BF), n, 4)
    a = pick(a, 1, y) + a_got.astype(F32)
    b = pick(b, 1, x) + b_got.astype(F32)
    ab = jnp.concatenate([a, b], axis=1)
    parts = [swap(pick(ab, 0, z ^ s).astype(BF), n, 8 * s) for s in (1, 2, 3)]
    return pick(ab, 0, z) + (parts[0].astype(F32) + parts[1].astype(F32) + parts[2].astype(F32))


def gather(attention, feedforward, biases, n, me):
    rows_each, rows_up, rows_down = 4 * D // n, D // (n // 2), FF // (n // 2)
    tail = jnp.pad(biases[None, None, :], ((0, 0), (0, 15), (0, 0)))
    own = jnp.concatenate([to_tiles(attention, rows_each, D), tail], axis=0)
    ga_all = lax.all_gather(own, AXES, axis=0)
    own = jnp.where(
        me < n // 2, to_tiles(feedforward, rows_up, FF), to_tiles(feedforward, rows_down, D)
    )
    return ga_all, lax.all_gather(own, AXES, axis=0)


def gather_any(attention, feedforward, biases):
    rows_each, rows_up, rows_down = 4 * D // PARTS, D // (PARTS // 2), FF // (PARTS // 2)
    full = lax.all_gather(attention, AXES, axis=0, tiled=True).reshape(PARTS, -1)
    tail = lax.all_gather(biases, AXES, axis=0, tiled=True).reshape(PARTS, 1, 1, 128)
    tail = jnp.pad(tail, ((0, 0), (0, 0), (0, 15), (0, 0)))
    squares = jax.vmap(lambda f: to_tiles(f, rows_each, D))(full)
    full = lax.all_gather(feedforward, AXES, axis=0, tiled=True).reshape(PARTS, -1)
    up = jax.vmap(lambda f: to_tiles(f, rows_up, FF))(full[: PARTS // 2])
    down = jax.vmap(lambda f: to_tiles(f, rows_down, D))(full[PARTS // 2 :])
    return jnp.concatenate([squares, tail], axis=1), jnp.concatenate([up, down])


def local(direct, tokens, cotangent, attention, feedforward, biases, gates, counts, lengths):
    me = lax.axis_index(AXES)
    n = PARTS
    rows_each, rows_up, rows_down = 4 * D // n, D // (n // 2), FF // (n // 2)
    if direct:
        ga_all, gf_all = gather(attention, feedforward, biases, n, me)
        place = jnp.stack([jnp.zeros_like(me), me % 2, me]).astype(jnp.int32)
    else:
        ga_all, gf_all = gather_any(attention, feedforward, biases)
        place = jnp.zeros((3,), jnp.int32)
    row = (ROWS, D)
    tiles = 4 * rows_each // 16
    ftiles = 4 * rows_down // 16
    wire = BF if direct else F32
    q, k, v, ctx, lse, branch, w, bias = call(
        partial(attend_body, n),
        [(row, BF)] * 4 + [((8, ROWS), F32), (row, F32), ((4, D, D), BF), ((1, 8 * D), F32)],
        [SMEM, SMEM, SMEM, VMEM, VMEM],
        [((2, ROWS, 128), BF), ((2, ROWS, 128), BF), ((ROWS, 128), F32)],
        4 << 30, 16 << 20, 56,
    )(counts, lengths, place, tokens, ga_all)
    layer, gm, gctx, ff_keep, ff_send, wo_grad, sums, gate = call(
        partial(feed_body, n),
        [(row, BF), (row, F32), (row, BF), ((n // 2, ftiles, 16, 128), F32), ((n // 2, ftiles, 16, 128), wire),
         ((D, D), F32), ((1, 8 * D), F32), ((2, D), F32)],
        [SMEM, SMEM] + [VMEM] * 7,
        [((D, FF), BF), ((FF, D), BF), (row, BF), (row, BF), (row, BF), ((ROWS, FF), BF), ((ROWS, FF), BF)],
        14 << 30, 30 << 20, 60,
    )(place, gates, tokens, branch, cotangent, ctx, w, bias, gf_all)
    if direct:
        ff_shard = scatter(ff_keep, ff_send, me, n)
    dq, dk, dv, keep, send = call(
        partial(back_body, n),
        [(row, BF)] * 3 + [((n // 2, tiles + 1, 16, 128), F32), ((n // 2, tiles + 1, 16, 128), wire)],
        [SMEM, SMEM, SMEM] + [VMEM] * 9,
        [((2, ROWS, 128), BF), ((2, ROWS, 128), BF), ((D, ROWS), BF), ((D, ROWS), F32), ((ROWS, 128), F32),
         ((ROWS, 128), F32), ((1, 8 * D), F32)],
        20 << 30, 16 << 20, 56,
    )(counts, lengths, place, tokens, q, k, v, gctx, lse, wo_grad, sums, gate)
    (input_grad,) = call(
        input_body, [(row, F32)], [VMEM] * 5, [], 2 << 30, 8 << 20, 32
    )(gm, dq, dk, dv, w)
    if direct:
        att_shard = scatter(keep, send, me, n)
        ff_grad = jnp.where(
            me < n // 2, from_tiles(ff_shard, rows_up, FF), from_tiles(ff_shard, rows_down, D)
        )
        att_grad = from_tiles(att_shard[:tiles], rows_each, D)
        last = att_shard[tiles]
        gate_grad = jnp.sum((last[1] + last[2] + last[3])[: 2 * n].reshape(n, 2), axis=0)
        return layer, input_grad, att_grad, ff_grad, last[0], gate_grad
    both = jnp.stack([ff_keep, ff_send], axis=1).reshape((n,) + ff_keep.shape[1:])
    up = jax.vmap(lambda t: from_tiles(t, rows_up, FF))(both[: n // 2]).reshape(-1)
    down = jax.vmap(lambda t: from_tiles(t, rows_down, D))(both[n // 2 :]).reshape(-1)
    ff_grad = lax.psum_scatter(jnp.concatenate([up, down]), AXES, scatter_dimension=0, tiled=True)
    both = jnp.stack([keep, send], axis=1).reshape((n,) + keep.shape[1:])
    flat = jax.vmap(lambda t: from_tiles(t, rows_each, D))(both[:, :tiles]).reshape(-1)
    att_grad = lax.psum_scatter(flat, AXES, scatter_dimension=0, tiled=True)
    bias_grad = lax.psum_scatter(both[:, tiles, 0].reshape(-1), AXES, scatter_dimension=0, tiled=True)
    last = both[0, tiles]
    gate_grad = lax.psum((last[1] + last[2] + last[3])[:2], AXES)
    return layer, input_grad, att_grad, ff_grad, bias_grad, gate_grad


def solution(mesh):
    direct = dict(mesh.shape) == {"dp": 8, "fsdp": 4}
    both = P(AXES)
    rows = P(AXES, None)
    return jax.shard_map(
        partial(local, direct),
        mesh=mesh,
        in_specs=(rows, rows, both, both, both, P(), rows, rows),
        out_specs=(rows, rows, both, both, both, P()),
        check_vma=False,
    )
```

time: 553 us -> 263 us (0.48)
  matrix products: 138 us -> 0 us
  Pallas kernels: 0 us -> 95 us
  blocking collectives: 84.2 us -> 0 us
  waiting for transfers between devices: 202 us -> 120 us
  local copies, waits for them, and re-layouts: 58.3 us -> 5.21 us
  other arithmetic: 49.3 us -> 7.69 us
  starting transfers between devices: 0.11 us -> 20.2 us
    unnamed x4 -> x2, waiting for transfers between devices: 181 us -> 0.03 us
    dot_general x32 -> x0, matrix products: 138 us -> none  [the longest x4 31.1 us: block_scores(): jnp.einsum('qhd,khd->hqk', queries, key_rows, preferred_element_type=jnp....]
    pallas_call x0 -> x4, Pallas kernels: none -> 95 us  [the longest x1 35.8 us: local(): call(partial(back_body, n), [(row, BF)] * 3 + [((n // 2, tiles + 1, 16, 1...]
    all_gather x2, waiting for transfers between devices: 20.3 us -> 94.8 us  [the longest x1 58.4 us: gather(): ga_all = lax.all_gather(own, AXES, axis=0)]
    all_gather x1 -> x0, blocking collectives: 43.2 us -> none  [local(): lax.all_gather(bias_params, ('dp', 'fsdp'), axis=0, tiled=True)]
    unnamed x1 -> x0, blocking collectives: 41 us -> none
    ppermute x0 -> x16, waiting for transfers between devices: none -> 25.6 us  [swap(): return lax.ppermute(x, AXES, [(i, i ^ bit) for i in range(n)])]
    convert_element_type x5 -> x2, other arithmetic: 21.8 us -> 0.09 us  [scatter(): parts = [swap(pick(ab, 0, z ^ s).astype(BF), n, 8 * s) for s in (1, 2, 3)]]
  transfers between devices with their start and end apart: 3 -> 18, of which waited for: 3 -> 12; matrix products, arithmetic and copies ran while one was open for 12% -> 3% of each run, Pallas kernels for 0% -> 12%
where the time goes in v1:
time: 263 us
  waiting for transfers between devices  120 us (46%)
  Pallas kernels  95 us (36%)
  starting transfers between devices  20.2 us (8%)
  between operations  14.3 us (5%)
  other arithmetic  7.69 us (3%)
  local copies, waits for them, and re-layouts  5.21 us (2%)
    all_gather x1, waiting for transfers between devices, gather(): ga_all = lax.all_gather(own, AXES, axis=0)  58.4 us
    all_gather x1, waiting for transfers between devices, gather(): return (ga_all, lax.all_gather(own, AXES, axis=0))  36.4 us
    pallas_call x1, Pallas kernels, local(): call(partial(back_body, n), [(row, BF)] * 3 + [((n // 2, tiles + 1, 16, 1...  35.8 us
    pallas_call x1, Pallas kernels, local(): call(partial(attend_body, n), [(row, BF)] * 4 + [((8, ROWS), F32), (row,...  28.1 us
    pallas_call x1, Pallas kernels, local(): call(partial(feed_body, n), [(row, BF), (row, F32), (row, BF), ((n // 2,...  27.3 us
    ppermute x16, waiting for transfers between devices, swap(): return lax.ppermute(x, AXES, [(i, i ^ bit) for i in range(n)])  25.6 us
    ppermute x16, starting transfers between devices, swap(): return lax.ppermute(x, AXES, [(i, i ^ bit) for i in range(n)])  20.1 us
  transfers between devices with their start and end apart: 18, of which 12 were waited for; matrix products, arithmetic and copies ran while one was open for 3% of the time, Pallas kernels for 12%

profile of v1, /device:TPU:0, one launch (start us, length us, event | category | flops | bytes accessed | tf_op | source)
XLA Modules:
  0.0 262.8 jit_solution(524783775072125457)
XLA Ops:
  7.2 0.9 copy.41
  8.1 1.3 fusion.34
  9.4 0.9 copy.43
  10.4 0.9 copy.42
  12.7 58.4 %all-gather.6.cloned.1.call-done = bf16[544,16,128]{2,1,0:T(8,128)(2,1)} async-done(((bf16[17,16,128]{2,1,0:T(8,128)(2,1)}), bf16[544,16,128]{2,1,0:T(8,128)(2,1)}) %all-gather.6.cloned.1.call-update) | async-done | bytes 2228240 | tf_op jit(solution)/shard_map/all_gather | solution.py:389
  71.1 28.1 %shard_map.127 = (bf16[1024,512]{1,0:T(8,128)(2,1)}, bf16[1024,512]{1,0:T(8,128)(2,1)}, bf16[1024,512]{1,0:T(8,128)(2,1)}, bf16[1024,512]{1,0:T(8,128)(2,1)}, f3...) custom-call(s32[1,3]{1,0:T(1,128)} %counts.3, s32[1,8]{1,0:T(1,128)} %lengths.3, ...), custom_call_target="tpu_custom_call" | custom-call | flops 4294967296 | bytes 16777216 | tf_op jit(solution)/shard_map/pallas_call | solution.py:422
  99.2 36.4 %all-gather.4.cloned.1.call-done.gathered = bf16[32,32,16,128]{3,2,1,0:T(8,128)(2,1)} async-done(((bf16[1,32,16,128]{3,2,1,0:T(8,128)(2,1)}), bf16[32,32,16,128]{3,2,1,0:T(8,128)(2,1)}) %all-gather.4.cloned.1.call-update) | async-done | bytes 4194320 | tf_op jit(solution)/shard_map/all_gather | solution.py:393
  135.7 27.3 %shard_map.128 = (bf16[1024,512]{1,0:T(8,128)(2,1)}, f32[1024,512]{1,0:T(8,128)}, bf16[1024,512]{1,0:T(8,128)(2,1)}, f32[16,32,16,128]{3,2,1,0:T(8,128)}, bf16[1...) custom-call(s32[3]{0:T(128)} %pad_add_fusion.place, f32[2]{0:T(128)} %gates.1, ...), custom_call_target="tpu_custom_call" | custom-call | flops 15032385536 | bytes 31457280 | tf_op jit(solution)/shard_map/pallas_call | solution.py:429
  162.9 35.8 %shard_map.129 = (bf16[1024,512]{1,0:T(8,128)(2,1)}, bf16[1024,512]{1,0:T(8,128)(2,1)}, bf16[1024,512]{1,0:T(8,128)(2,1)}, f32[16,17,16,128]{3,2,1,0:T(8,128)}, bf16[16,17,16,128]{3,2,1,0:T(8,128)(2,1)}) custom-call(s32[1,3]{1,0:T(1,128)} %counts.3, s32[1,8]{1,0:T(1,128)} %lengths.3, s32[3]{0:T(128)} %pad_add_fusion.place, bf16[1024,512]{1,0:T(8,128)(2,1)} %tok.5, ...), custom_call_target="tpu_custom_call" | custom-call | flops 21474836480 | bytes 16777216 | tf_op jit(solution)/shard_map/pallas_call | solution.py:439
  199.3 2.5 collective-permute-done
  201.7 2.0 convert_add_fusion.1
  203.9 1.3 collective-permute-start.1
  205.8 3.7 %shard_map.130 = f32[1024,512]{1,0:T(8,128)} custom-call(f32[1024,512]{1,0:T(8,128)S(1)} %copy-done.1, bf16[1024,512]{1,0:T(8,128)(2,1)S(1)} %copy-done.2, bf16[1024,512]{1,0:T(8,128)(2,1)S(1)} %copy-done.3, bf16[1024,512]{1,0:T(8,128)(2,1)S(1)} %copy-done.4, bf16[4,512,512]{2,1,0:T(8,128)(2,1)S(1)} %copy-done), custom_call_target="tpu_custom_call" | custom-call | flops 2147483648 | bytes 8388608 | tf_op jit(solution)/shard_map/pallas_call | solution.py:447
  209.7 1.5 collective-permute-start.3
  211.3 1.2 collective-permute-done.1
  212.5 1.5 collective-permute-start.2
  214.1 5.5 %collective-permute-done.3 = bf16[4,2,9,16,128]{4,3,2,0,1:T(8,128)(2,1)S(1)} collective-permute-done((bf16[4,2,9,16,128]{4,3,2,0,1:T(8,128)(2,1)S(1)}, bf16[4,2,9,16,128]{4,3,2,0,1:T(8,128)(2,1)S(1)}, u32[]{:S(2)}, u32[]{:S(2)}) %collective-permute-start.3) | collective-permute-done | bytes 294944 | tf_op jit(solution)/shard_map/ppermute | solution.py:358
  219.7 1.3 collective-permute-start.4
  223.0 1.5 collective-permute-start.9
  224.5 1.4 collective-permute-done.4
  226.0 1.5 collective-permute-start.5
  227.5 1.0 collective-permute-start.6
  228.5 1.9 collective-permute-start.7
  230.5 4.0 %collective-permute-done.11 = bf16[4,2,16,16,128]{4,3,2,0,1:T(8,128)(2,1)S(1)} collective-permute-done((bf16[4,2,16,16,128]{4,3,2,0,1:T(8,128)(2,1)S(1)}, bf16[4,2,16,16,128]{4,3,2,0,1:T(8,128)(2,1)S(1)}, u32[]{:S(2)}, u32[]{:S(2)}) %collective-permute-start.11) | collective-permute-done | bytes 524320 | tf_op jit(solution)/shard_map/ppermute | solution.py:358
  235.4 2.0 collective-permute-done.9
  237.6 1.8 collective-permute-start.10
  239.4 2.3 collective-permute-done.12
  241.8 2.2 collective-permute-done.10
  244.2 1.5 collective-permute-start.13
  245.7 1.0 collective-permute-start.14
  246.7 1.9 collective-permute-start.15
  250.8 4.2 %collective-permute-done.14 = bf16[32,16,128]{2,1,0:T(8,128)(2,1)S(1)} collective-permute-done((bf16[32,16,128]{2,1,0:T(8,128)(2,1)S(1)}, bf16[32,16,128]{2,1,0:T(8,128)(2,1)S(1)}, u32[]{:S(2)}, u32[]{:S(2)}) %collective-permute-start.14) | collective-permute-done | bytes 131104 | tf_op jit(solution)/shard_map/ppermute | solution.py:358
  (62 shorter events, 9.5 us)
Async XLA Ops:
  7.2 63.9 %all-gather.6.cloned.1.call-start = ((), (), s32[]{:S(2)}) async-start(), calls=%async_computation.1 | async-start | bytes 2297856 | tf_op jit(solution)/shard_map/all_gather | solution.py:389
  9.4 126.3 %all-gather.4.cloned.1.call-start = ((), (), s32[]{:S(2)}) async-start(), calls=%async_computation | async-start | bytes 4325376 | tf_op jit(solution)/shard_map/all_gather | solution.py:393
  198.7 3.0 %collective-permute-start = (bf16[16,17,16,128]{3,2,1,0:T(8,128)(2,1)}, bf16[16,17,16,128]{3,2,1,0:T(8,128)(2,1)S(1)}, u32[]{:S(2)}, u32[]{:S(2)}) collective-permute-start(bf16[16,17,16,128]{3,2,1,0:T(8,128)(2,1)} %get-tuple-element.45), channel_id=1, source_target_pairs={{0,1},{1,0},{2,3},{3,2},{4,5},{5,4},{6,7},{7,6},{8,9},{9,8},{10,11... | collective-permute-start | bytes 3342344 | tf_op jit(solution)/shard_map/ppermute | solution.py:358
  199.0 22.0 %collective-permute-start.8 = (bf16[16,32,16,128]{3,2,1,0:T(8,128)(2,1)}, bf16[16,32,16,128]{3,2,1,0:T(8,128)(2,1)S(1)}, u32[]{:S(2)}, u32[]{:S(2)}) collective-permute-start(bf16[16,32,16,128]{3,2,1,0:T(8,128)(2,1)} %get-tuple-element.47), channel_id=1, source_target_pairs={{0,1},{1,0},{2,3},{3,2},{4,5},{5,4},{6,7},{7,6},{8,9},{9,8},{10,11... | collective-permute-start | bytes 6291464 | tf_op jit(solution)/shard_map/ppermute | solution.py:358
  201.7 3.5 %copy-start.1 = (f32[1024,512]{1,0:T(8,128)S(1)}, f32[1024,512]{1,0:T(8,128)}, u32[]{:S(2)}) copy-start(f32[1024,512]{1,0:T(8,128)} %get-tuple-element.32.gm) | copy-start | bytes 6291460
  201.7 3.5 %copy-start.2 = (bf16[1024,512]{1,0:T(8,128)(2,1)S(1)}, bf16[1024,512]{1,0:T(8,128)(2,1)}, u32[]{:S(2)}) copy-start(bf16[1024,512]{1,0:T(8,128)(2,1)} %get-tuple-element.41.dq) | copy-start | bytes 3145732
  201.7 3.5 %copy-start.3 = (bf16[1024,512]{1,0:T(8,128)(2,1)S(1)}, bf16[1024,512]{1,0:T(8,128)(2,1)}, u32[]{:S(2)}) copy-start(bf16[1024,512]{1,0:T(8,128)(2,1)} %get-tuple-element.42.dk) | copy-start | bytes 3145732
  201.7 3.5 %copy-start.4 = (bf16[1024,512]{1,0:T(8,128)(2,1)S(1)}, bf16[1024,512]{1,0:T(8,128)(2,1)}, u32[]{:S(2)}) copy-start(bf16[1024,512]{1,0:T(8,128)(2,1)} %get-tuple-element.43.dv) | copy-start | bytes 3145732
  203.7 2.1 copy-start
  203.9 8.5 %collective-permute-start.1 = (bf16[4,2,8,16,128]{4,3,2,0,1:T(8,128)(2,1)S(1)}, bf16[4,2,8,16,128]{4,3,2,0,1:T(8,128)(2,1)S(1)}, u32[]{:S(2)}, u32[]{:S(2)}) collective-permute-start(bf16[4,2,8,16,128]{4,3,2,0,1:T(8,128)(2,1)S(1)} %fusion.9), channel_id=1, source_target_pairs={{0,4},{1,5},{2,6},{3,7},{4,0},{5,1},{6,2},{7,3},{8,12},{9,13},{10,... | collective-permute-start | bytes 786440 | tf_op jit(solution)/shard_map/ppermute | solution.py:358
  209.5 11.5 %copy-start.5 = (f32[16,32,16,128]{3,2,1,0:T(8,128)S(1)}, f32[16,32,16,128]{3,2,1,0:T(8,128)}, u32[]{:S(2)}) copy-start(f32[16,32,16,128]{3,2,1,0:T(8,128)} %get-tuple-element.46) | copy-start | bytes 12582916
  209.7 9.9 %collective-permute-start.3 = (bf16[4,2,9,16,128]{4,3,2,0,1:T(8,128)(2,1)S(1)}, bf16[4,2,9,16,128]{4,3,2,0,1:T(8,128)(2,1)S(1)}, u32[]{:S(2)}, u32[]{:S(2)}) collective-permute-start(bf16[4,2,9,16,128]{4,3,2,0,1:T(8,128)(2,1)S(1)} %fusion.6), channel_id=1, source_target_pairs={{0,2},{1,3},{2,0},{3,1},{4,6},{5,7},{6,4},{7,5},{8,10},{9,11},{10,... | collective-permute-start | bytes 884744 | tf_op jit(solution)/shard_map/ppermute | solution.py:358
  212.5 10.3 %collective-permute-start.2 = (bf16[4,8,16,128]{3,2,1,0:T(8,128)(2,1)S(1)}, bf16[4,8,16,128]{3,2,1,0:T(8,128)(2,1)S(1)}, u32[]{:S(2)}, u32[]{:S(2)}) collective-permute-start(bf16[4,8,16,128]{3,2,1,0:T(8,128)(2,1)S(1)} %fusion.30), channel_id=1, source_target_pairs={{0,2},{1,3},{2,0},{3,1},{4,6},{5,7},{6,4},{7,5},{8,10},{9,11},{10,... | collective-permute-start | bytes 393224 | tf_op jit(solution)/shard_map/ppermute | solution.py:358
  219.7 6.2 %collective-permute-start.4 = (bf16[4,9,16,128]{3,2,1,0:T(8,128)(2,1)S(1)}, bf16[4,9,16,128]{3,2,1,0:T(8,128)(2,1)S(1)}, u32[]{:S(2)}, u32[]{:S(2)}) collective-permute-start(bf16[4,9,16,128]{3,2,1,0:T(8,128)(2,1)S(1)} %fusion.19), channel_id=1, source_target_pairs={{0,4},{1,5},{2,6},{3,7},{4,0},{5,1},{6,2},{7,3},{8,12},{9,13},{10,... | collective-permute-start | bytes 442376 | tf_op jit(solution)/shard_map/ppermute | solution.py:358
  222.0 12.4 %collective-permute-start.11 = (bf16[4,2,16,16,128]{4,3,2,0,1:T(8,128)(2,1)S(1)}, bf16[4,2,16,16,128]{4,3,2,0,1:T(8,128)(2,1)S(1)}, u32[]{:S(2)}, u32[]{:S(2)}) collective-permute-start(bf16[4,2,16,16,128]{4,3,2,0,1:T(8,128)(2,1)S(1)} %fusion.4), channel_id=1, source_target_pairs={{0,2},{1,3},{2,0},{3,1},{4,6},{5,7},{6,4},{7,5},{8,10},{9,11},{10,... | collective-permute-start | bytes 1572872 | tf_op jit(solution)/shard_map/ppermute | solution.py:358
  223.0 14.5 %collective-permute-start.9 = (bf16[4,2,16,16,128]{4,3,2,0,1:T(8,128)(2,1)S(1)}, bf16[4,2,16,16,128]{4,3,2,0,1:T(8,128)(2,1)S(1)}, u32[]{:S(2)}, u32[]{:S(2)}) collective-permute-start(bf16[4,2,16,16,128]{4,3,2,0,1:T(8,128)(2,1)S(1)} %fusion.3), channel_id=1, source_target_pairs={{0,4},{1,5},{2,6},{3,7},{4,0},{5,1},{6,2},{7,3},{8,12},{9,13},{10,... | collective-permute-start | bytes 1572872 | tf_op jit(solution)/shard_map/ppermute | solution.py:358
  226.0 13.4 %collective-permute-start.5 = (bf16[17,16,128]{2,1,0:T(8,128)(2,1)S(1)}, bf16[17,16,128]{2,1,0:T(8,128)(2,1)S(1)}, u32[]{:S(2)}, u32[]{:S(2)}) collective-permute-start(bf16[17,16,128]{2,1,0:T(8,128)(2,1)S(1)} %get-tuple-element.53), channel_id=1, source_target_pairs={{0,8},{1,9},{2,10},{3,11},{4,12},{5,13},{6,14},{7,15},{8,0},{9,1},... | collective-permute-start | bytes 208904 | tf_op jit(solution)/shard_map/ppermute | solution.py:358
  227.5 11.9 %collective-permute-start.6 = (bf16[17,16,128]{2,1,0:T(8,128)(2,1)S(1)}, bf16[17,16,128]{2,1,0:T(8,128)(2,1)S(1)}, u32[]{:S(2)}, u32[]{:S(2)}) collective-permute-start(bf16[17,16,128]{2,1,0:T(8,128)(2,1)S(1)} %get-tuple-element.54), channel_id=1, source_target_pairs={{0,16},{1,17},{2,18},{3,19},{4,20},{5,21},{6,22},{7,23},{8,24},{9,... | collective-permute-start | bytes 208904 | tf_op jit(solution)/shard_map/ppermute | solution.py:358
  228.5 10.9 %collective-permute-start.7 = (bf16[17,16,128]{2,1,0:T(8,128)(2,1)S(1)}, bf16[17,16,128]{2,1,0:T(8,128)(2,1)S(1)}, u32[]{:S(2)}, u32[]{:S(2)}) collective-permute-start(bf16[17,16,128]{2,1,0:T(8,128)(2,1)S(1)} %get-tuple-element.55), channel_id=1, source_target_pairs={{0,24},{1,25},{2,26},{3,27},{4,28},{5,29},{6,30},{7,31},{8,16},{9,... | collective-permute-start | bytes 208904 | tf_op jit(solution)/shard_map/ppermute | solution.py:358
  234.6 7.2 %collective-permute-start.12 = (bf16[4,16,16,128]{3,2,1,0:T(8,128)(2,1)S(1)}, bf16[4,16,16,128]{3,2,1,0:T(8,128)(2,1)S(1)}, u32[]{:S(2)}, u32[]{:S(2)}) collective-permute-start(bf16[4,16,16,128]{3,2,1,0:T(8,128)(2,1)S(1)} %fusion.8), channel_id=1, source_target_pairs={{0,4},{1,5},{2,6},{3,7},{4,0},{5,1},{6,2},{7,3},{8,12},{9,13},{10,... | collective-permute-start | bytes 786440 | tf_op jit(solution)/shard_map/ppermute | solution.py:358
  237.6 6.4 %collective-permute-start.10 = (bf16[4,16,16,128]{3,2,1,0:T(8,128)(2,1)S(1)}, bf16[4,16,16,128]{3,2,1,0:T(8,128)(2,1)S(1)}, u32[]{:S(2)}, u32[]{:S(2)}) collective-permute-start(bf16[4,16,16,128]{3,2,1,0:T(8,128)(2,1)S(1)} %fusion.7), channel_id=1, source_target_pairs={{0,2},{1,3},{2,0},{3,1},{4,6},{5,7},{6,4},{7,5},{8,10},{9,11},{10,... | collective-permute-start | bytes 786440 | tf_op jit(solution)/shard_map/ppermute | solution.py:358
  244.2 6.7 %collective-permute-start.13 = (bf16[32,16,128]{2,1,0:T(8,128)(2,1)S(1)}, bf16[32,16,128]{2,1,0:T(8,128)(2,1)S(1)}, u32[]{:S(2)}, u32[]{:S(2)}) collective-permute-start(bf16[32,16,128]{2,1,0:T(8,128)(2,1)S(1)} %get-tuple-element.50), channel_id=1, source_target_pairs={{0,8},{1,9},{2,10},{3,11},{4,12},{5,13},{6,14},{7,15},{8,0},{9,1},... | collective-permute-start | bytes 393224 | tf_op jit(solution)/shard_map/ppermute | solution.py:358
  245.7 9.3 %collective-permute-start.14 = (bf16[32,16,128]{2,1,0:T(8,128)(2,1)S(1)}, bf16[32,16,128]{2,1,0:T(8,128)(2,1)S(1)}, u32[]{:S(2)}, u32[]{:S(2)}) collective-permute-start(bf16[32,16,128]{2,1,0:T(8,128)(2,1)S(1)} %get-tuple-element.51), channel_id=1, source_target_pairs={{0,16},{1,17},{2,18},{3,19},{4,20},{5,21},{6,22},{7,23},{8,24},{9,... | collective-permute-start | bytes 393224 | tf_op jit(solution)/shard_map/ppermute | solution.py:358
  246.7 8.3 %collective-permute-start.15 = (bf16[32,16,128]{2,1,0:T(8,128)(2,1)S(1)}, bf16[32,16,128]{2,1,0:T(8,128)(2,1)S(1)}, u32[]{:S(2)}, u32[]{:S(2)}) collective-permute-start(bf16[32,16,128]{2,1,0:T(8,128)(2,1)S(1)} %get-tuple-element.52), channel_id=1, source_target_pairs={{0,24},{1,25},{2,26},{3,27},{4,28},{5,29},{6,30},{7,31},{8,16},{9,... | collective-permute-start | bytes 393224 | tf_op jit(solution)/shard_map/ppermute | solution.py:358
Sparse Core Ops, SparseCore 0:
  11.5 59.6 all-gather.5
  74.5 61.0 all-gather.3

commit v2 on v1

--- a/solution.py
+++ b/solution.py
@@ -79,25 +79,27 @@
 
 
 def attend_body(
-    n, counts, lengths, place, tok, gathered, q_out, k_out, v_out, ctx_out, lse_out, branch_out,
-    w_out, bias_out, keys_mask, rows_mask, lse_cols,
+    n, counts, lengths, place, tok, *refs
 ):
+    gathered, refs = refs[:8], refs[8:]
+    (q_out, k_out, v_out, ctx_out, lse_out, branch_out, w_out, bias_out, keys_mask, rows_mask, lse_cols) = refs
     rows_each = D * 4 // n
     tiles = rows_each // 16
 
-    def assemble(o, _):
-        piece = o ^ place[0]
-        square, row = o // (n // 4), (o % (n // 4)) * rows_each
-        for i in range(tiles):
-            for j in range(4):
-                w_out[square, pl.ds(pl.multiple_of(row + 16 * i, 16), 16), 128 * j : 128 * j + 128] = (
-                    gathered[piece, 4 * i + j]
-                )
-        tail = gathered[piece, 4 * tiles].astype(F32)
-        bias_out[0:1, pl.ds(pl.multiple_of(o * 128, 128), 128)] = tail[0:1]
-        return 0
-
-    lax.fori_loop(0, n, assemble, 0)
+    def assemble(z, _):
+        for d in range(8):
+            o = (8 * z + d) ^ place[0]
+            square, row = o // (n // 4), (o % (n // 4)) * rows_each
+            for i in range(tiles):
+                for j in range(4):
+                    w_out[square, pl.ds(pl.multiple_of(row + 16 * i, 16), 16), 128 * j : 128 * j + 128] = (
+                        gathered[d][z, 4 * i + j]
+                    )
+            tail = gathered[d][z, 4 * tiles].astype(F32)
+            bias_out[0:1, pl.ds(pl.multiple_of(o * 128, 128), 128)] = tail[0:1]
+        return 0
+
+    lax.fori_loop(0, n // 8, assemble, 0)
     slot_masks(counts, lengths, keys_mask, rows_mask)
 
     def project(r, _):
@@ -153,34 +155,36 @@
 
 
 def feed_body(
-    n, place, gates, tok, branch, cot, ctx, w_out, bias, gathered,
-    layer_out, gm_out, gctx_out, keep_out, send_out, wo_out, sums_out, gate_out,
-    w1, w2, mlow, gbr, gs_all, active_all, gh_all,
+    n, place, gates, tok, branch, cot, ctx, w_out, bias, *refs
 ):
+    gathered, refs = refs[:8], refs[8:]
+    (layer_out, gm_out, gctx_out, keep_out, send_out, wo_out, sums_out, gate_out) = refs[:8]
+    (w1, w2, mlow, gbr, gs_all, active_all, gh_all) = refs[8:]
     rows_up = D // (n // 2)
     rows_down = FF // (n // 2)
     tiles = rows_down // 16 * 4
 
-    def assemble_up(o, _):
-        piece = o ^ place[0]
-        for i in range(rows_up // 16):
-            for j in range(16):
-                w1[pl.ds(pl.multiple_of(o * rows_up + 16 * i, 16), 16), 128 * j : 128 * j + 128] = (
-                    gathered[piece, 16 * i + j]
-                )
-        return 0
-
-    def assemble_down(o, _):
-        piece = (o + n // 2) ^ place[0]
-        for i in range(rows_down // 16):
-            for j in range(4):
-                w2[pl.ds(pl.multiple_of(o * rows_down + 16 * i, 16), 16), 128 * j : 128 * j + 128] = (
-                    gathered[piece, 4 * i + j]
-                )
-        return 0
-
-    lax.fori_loop(0, n // 2, assemble_up, 0)
-    lax.fori_loop(0, n // 2, assemble_down, 0)
+    def assemble(z, _):
+        for d in range(8):
+            o = (8 * z + d) ^ place[0]
+
+            @pl.when(o < n // 2)
+            def _():
+                for i in range(rows_up // 16):
+                    for j in range(16):
+                        row = pl.ds(pl.multiple_of(o * rows_up + 16 * i, 16), 16)
+                        w1[row, 128 * j : 128 * j + 128] = gathered[d][z, 16 * i + j]
+
+            @pl.when(o >= n // 2)
+            def _():
+                for i in range(rows_down // 16):
+                    for j in range(4):
+                        row = pl.ds(pl.multiple_of((o - n // 2) * rows_down + 16 * i, 16), 16)
+                        w2[row, 128 * j : 128 * j + 128] = gathered[d][z, 4 * i + j]
+
+        return 0
+
+    lax.fori_loop(0, n // 8, assemble, 0)
     ga, gf = gates[0], gates[1]
     sums_out[...] = jnp.zeros_like(sums_out)
     c1 = 0.7978845608028654
@@ -382,15 +386,20 @@
     return pick(ab, 0, z) + (parts[0].astype(F32) + parts[1].astype(F32) + parts[2].astype(F32))
 
 
+def spread(own, n):
+    stack = jnp.stack([own] + [swap(own, n, 8 * z) for z in (1, 2, 3)])
+    chips = [stack] + [swap(stack, n, bits) for bits in (2, 4, 6)]
+    return [part for chip in chips for part in (chip, swap(chip, n, 1))]
+
+
 def gather(attention, feedforward, biases, n, me):
     rows_each, rows_up, rows_down = 4 * D // n, D // (n // 2), FF // (n // 2)
     tail = jnp.pad(biases[None, None, :], ((0, 0), (0, 15), (0, 0)))
-    own = jnp.concatenate([to_tiles(attention, rows_each, D), tail], axis=0)
-    ga_all = lax.all_gather(own, AXES, axis=0)
-    own = jnp.where(
+    own_a = jnp.concatenate([to_tiles(attention, rows_each, D), tail], axis=0)
+    own_f = jnp.where(
         me < n // 2, to_tiles(feedforward, rows_up, FF), to_tiles(feedforward, rows_down, D)
     )
-    return ga_all, lax.all_gather(own, AXES, axis=0)
+    return spread(own_a, n), spread(own_f, n)
 
 
 def gather_any(attention, feedforward, biases):
@@ -402,7 +411,8 @@
     full = lax.all_gather(feedforward, AXES, axis=0, tiled=True).reshape(PARTS, -1)
     up = jax.vmap(lambda f: to_tiles(f, rows_up, FF))(full[: PARTS // 2])
     down = jax.vmap(lambda f: to_tiles(f, rows_down, D))(full[PARTS // 2 :])
-    return jnp.concatenate([squares, tail], axis=1), jnp.concatenate([up, down])
+    pieces = jnp.concatenate([squares, tail], axis=1), jnp.concatenate([up, down])
+    return [[p.reshape((4, 8) + p.shape[1:])[:, d] for d in range(8)] for p in pieces]
 
 
 def local(direct, tokens, cotangent, attention, feedforward, biases, gates, counts, lengths):
@@ -411,7 +421,7 @@
     rows_each, rows_up, rows_down = 4 * D // n, D // (n // 2), FF // (n // 2)
     if direct:
         ga_all, gf_all = gather(attention, feedforward, biases, n, me)
-        place = jnp.stack([jnp.zeros_like(me), me % 2, me]).astype(jnp.int32)
+        place = jnp.stack([me, me % 2, me]).astype(jnp.int32)
     else:
         ga_all, gf_all = gather_any(attention, feedforward, biases)
         place = jnp.zeros((3,), jnp.int32)
@@ -422,18 +432,18 @@
     q, k, v, ctx, lse, branch, w, bias = call(
         partial(attend_body, n),
         [(row, BF)] * 4 + [((8, ROWS), F32), (row, F32), ((4, D, D), BF), ((1, 8 * D), F32)],
-        [SMEM, SMEM, SMEM, VMEM, VMEM],
+        [SMEM, SMEM, SMEM] + [VMEM] * 9,
         [((2, ROWS, 128), BF), ((2, ROWS, 128), BF), ((ROWS, 128), F32)],
         4 << 30, 16 << 20, 56,
-    )(counts, lengths, place, tokens, ga_all)
+    )(counts, lengths, place, tokens, *ga_all)
     layer, gm, gctx, ff_keep, ff_send, wo_grad, sums, gate = call(
         partial(feed_body, n),
         [(row, BF), (row, F32), (row, BF), ((n // 2, ftiles, 16, 128), F32), ((n // 2, ftiles, 16, 128), wire),
          ((D, D), F32), ((1, 8 * D), F32), ((2, D), F32)],
-        [SMEM, SMEM] + [VMEM] * 7,
+        [SMEM, SMEM] + [VMEM] * 14,
         [((D, FF), BF), ((FF, D), BF), (row, BF), (row, BF), (row, BF), ((ROWS, FF), BF), ((ROWS, FF), BF)],
         14 << 30, 30 << 20, 60,
-    )(place, gates, tokens, branch, cotangent, ctx, w, bias, gf_all)
+    )(place, gates, tokens, branch, cotangent, ctx, w, bias, *gf_all)
     if direct:
         ff_shard = scatter(ff_keep, ff_send, me, n)
     dq, dk, dv, keep, send = call(

time: 263 us -> 202 us (0.77)
  waiting for transfers between devices: 120 us -> 52.2 us
  starting transfers between devices: 20.2 us -> 40.5 us
  between operations: 14.3 us -> 1.08 us
    all_gather x2 -> x0, waiting for transfers between devices: 94.8 us -> none  [the longest x1 58.4 us: gather(): ga_all = lax.all_gather(own, AXES, axis=0)]
    ppermute x16 -> x36, waiting for transfers between devices: 25.6 us -> 52.2 us  [swap(): return lax.ppermute(x, AXES, [(i, i ^ bit) for i in range(n)])]
    ppermute x16 -> x36, starting transfers between devices: 20.1 us -> 40.5 us  [swap(): return lax.ppermute(x, AXES, [(i, i ^ bit) for i in range(n)])]
  transfers between devices with their start and end apart: 18 -> 36, of which waited for: 12 -> 19; matrix products, arithmetic and copies ran while one was open for 3% -> 4% of each run, Pallas kernels for 12% -> 16%
where the time goes in v2:
time: 202 us; the launch traced here: 201 us
  Pallas kernels  95.2 us (47%)
  waiting for transfers between devices  52.2 us (26%)
  starting transfers between devices  40.5 us (20%)
  other arithmetic  6.55 us (3%)
  local copies, waits for them, and re-layouts  5.9 us (3%)
    ppermute x36, waiting for transfers between devices, swap(): return lax.ppermute(x, AXES, [(i, i ^ bit) for i in range(n)])  52.2 us
    ppermute x36, starting transfers between devices, swap(): return lax.ppermute(x, AXES, [(i, i ^ bit) for i in range(n)])  40.5 us
    pallas_call x1, Pallas kernels, local(): call(partial(back_body, n), [(row, BF)] * 3 + [((n // 2, tiles + 1, 16, 1...  35.8 us
    pallas_call x1, Pallas kernels, local(): call(partial(attend_body, n), [(row, BF)] * 4 + [((8, ROWS), F32), (row,...  28.1 us
    pallas_call x1, Pallas kernels, local(): call(partial(feed_body, n), [(row, BF), (row, F32), (row, BF), ((n // 2,...  27.5 us
  transfers between devices with their start and end apart: 36, of which 19 were waited for; matrix products, arithmetic and copies ran while one was open for 4% of the time, Pallas kernels for 16%

profile of v2, /device:TPU:0, one launch (start us, length us, event | category | flops | bytes accessed | tf_op | source)
XLA Modules:
  0.0 201.4 jit_solution(17117595530312096160)
XLA Ops:
  2.2 3.1 %collective-permute-start = (bf16[17,16,128]{2,1,0:T(8,128)(2,1)S(1)}, bf16[17,16,128]{2,1,0:T(8,128)(2,1)S(1)}, u32[]{:S(2)}, u32[]{:S(2)}) collective-permute-start(bf16[17,16,128]{2,1,0:T(8,128)(2,1)S(1)} %get-tuple-element.59), channel_id=1, source_target_pairs={{0,8},{1,9},{2,10},{3,11},{4,12},{5,13},{6,14},{7,15},{8,0},{9,1},... | collective-permute-start | bytes 208904 | tf_op jit(solution)/shard_map/ppermute | solution.py:362
  5.3 2.6 %collective-permute-start.1 = (bf16[17,16,128]{2,1,0:T(8,128)(2,1)S(1)}, bf16[17,16,128]{2,1,0:T(8,128)(2,1)S(1)}, u32[]{:S(2)}, u32[]{:S(2)}) collective-permute-start(bf16[17,16,128]{2,1,0:T(8,128)(2,1)S(1)} %get-tuple-element.59), channel_id=1, source_target_pairs={{0,16},{1,17},{2,18},{3,19},{4,20},{5,21},{6,22},{7,23},{8,24},{9,... | collective-permute-start | bytes 208904 | tf_op jit(solution)/shard_map/ppermute | solution.py:362
  10.7 3.5 %collective-permute-start.11 = (bf16[32,16,128]{2,1,0:T(8,128)(2,1)S(1)}, bf16[32,16,128]{2,1,0:T(8,128)(2,1)S(1)}, u32[]{:S(2)}, u32[]{:S(2)}) collective-permute-start(bf16[32,16,128]{2,1,0:T(8,128)(2,1)S(1)} %bitcast_select_fusion), channel_id=1, source_target_pairs={{0,16},{1,17},{2,18},{3,19},{4,20},{5,21},{6,22},{7,23},{8,24},{9,... | collective-permute-start | bytes 393224 | tf_op jit(solution)/shard_map/ppermute | solution.py:362
  14.5 1.6 collective-permute-start.4
  16.1 1.5 collective-permute-start.6
  18.1 2.4 %collective-permute-start.8 = (bf16[4,17,16,128]{3,2,1,0:T(8,128)(2,1)S(1)}, bf16[4,17,16,128]{3,2,1,0:T(8,128)(2,1)}, u32[]{:S(2)}, u32[]{:S(2)}) collective-permute-start(bf16[4,17,16,128]{3,2,1,0:T(8,128)(2,1)S(1)} %pad_maximum_fusion.1.refs_0_), channel_id=1, source_target_pairs={{0,6},{1,7},{2,4},{3,5},{4,2},{5,3},{6,0},{7,1},{8,14},{9,15},{10,... | collective-permute-start | bytes 835592 | tf_op jit(solution)/shard_map/ppermute | solution.py:362
  20.5 3.5 %collective-permute-done.11 = bf16[32,16,128]{2,1,0:T(8,128)(2,1)S(1)} collective-permute-done((bf16[32,16,128]{2,1,0:T(8,128)(2,1)S(1)}, bf16[32,16,128]{2,1,0:T(8,128)(2,1)S(1)}, u32[]{:S(2)}, u32[]{:S(2)}) %collective-permute-start.11) | collective-permute-done | bytes 131104 | tf_op jit(solution)/shard_map/ppermute | solution.py:362
  24.2 1.6 collective-permute-start.14
  25.8 1.5 collective-permute-start.16
  30.8 9.6 %collective-permute-done.14.refs_2_ = bf16[4,32,16,128]{3,2,1,0:T(8,128)(2,1)S(1)} collective-permute-done((bf16[4,32,16,128]{3,2,1,0:T(8,128)(2,1)S(1)}, bf16[4,32,16,128]{3,2,1,0:T(8,128)(2,1)S(1)}, u32[]{:S(2)}, u32[]{:S(2)}) %collective-permute-start.14) | collective-permute-done | bytes 524320 | tf_op jit(solution)/shard_map/ppermute | solution.py:362
  41.0 10.1 %collective-permute-done.18.refs_6_ = bf16[4,32,16,128]{3,2,1,0:T(8,128)(2,1)S(1)} collective-permute-done((bf16[4,32,16,128]{3,2,1,0:T(8,128)(2,1)S(1)}, bf16[4,32,16,128]{3,2,1,0:T(8,128)(2,1)S(1)}, u32[]{:S(2)}, u32[]{:S(2)}) %collective-permute-start.18) | collective-permute-done | bytes 524320 | tf_op jit(solution)/shard_map/ppermute | solution.py:362
  51.8 28.1 %shard_map.127 = (bf16[1024,512]{1,0:T(8,128)(2,1)}, bf16[1024,512]{1,0:T(8,128)(2,1)}, bf16[1024,512]{1,0:T(8,128)(2,1)}, bf16[1024,512]{1,0:T(8,128)(2,1)}, f3...) custom-call(s32[1,3]{1,0:T(1,128)} %counts.3, s32[1,8]{1,0:T(1,128)} %lengths.3, ...), custom_call_target="tpu_custom_call" | custom-call | flops 4294967296 | bytes 16777216 | tf_op jit(solution)/shard_map/pallas_call | solution.py:432
  80.9 27.5 %shard_map.128 = (bf16[1024,512]{1,0:T(8,128)(2,1)}, f32[1024,512]{1,0:T(8,128)}, bf16[1024,512]{1,0:T(8,128)(2,1)}, f32[16,32,16,128]{3,2,1,0:T(8,128)}, bf16[1...) custom-call(s32[3]{0:T(128)} %pad_add_fusion.place, f32[2]{0:T(128)} %gates.1, ...), custom_call_target="tpu_custom_call" | custom-call | flops 15032385536 | bytes 31457280 | tf_op jit(solution)/shard_map/pallas_call | solution.py:439
  108.5 35.8 %shard_map.129 = (bf16[1024,512]{1,0:T(8,128)(2,1)}, bf16[1024,512]{1,0:T(8,128)(2,1)}, bf16[1024,512]{1,0:T(8,128)(2,1)}, f32[16,17,16,128]{3,2,1,0:T(8,128)}, bf16[16,17,16,128]{3,2,1,0:T(8,128)(2,1)}) custom-call(s32[1,3]{1,0:T(1,128)} %counts.3, s32[1,8]{1,0:T(1,128)} %lengths.3, s32[3]{0:T(128)} %pad_add_fusion.place, bf16[1024,512]{1,0:T(8,128)(2,1)} %tok.5, ...), custom_call_target="tpu_custom_call" | custom-call | flops 21474836480 | bytes 16777216 | tf_op jit(solution)/shard_map/pallas_call | solution.py:449
  144.8 2.5 %collective-permute-done.20 = bf16[16,17,16,128]{3,2,1,0:T(8,128)(2,1)S(1)} collective-permute-done((bf16[16,17,16,128]{3,2,1,0:T(8,128)(2,1)}, bf16[16,17,16,128]{3,2,1,0:T(8,128)(2,1)S(1)}, u32[]{:S(2)}, u32[]{:S(2)}) %collective-permute-start.20) | collective-permute-done | bytes 1114144 | tf_op jit(solution)/shard_map/ppermute | solution.py:362
  147.4 2.0 convert_add_fusion.1
  149.5 1.6 collective-permute-start.21
  151.4 3.7 %shard_map.130 = f32[1024,512]{1,0:T(8,128)} custom-call(f32[1024,512]{1,0:T(8,128)S(1)} %copy-done.1, bf16[1024,512]{1,0:T(8,128)(2,1)S(1)} %copy-done.2, bf16[1024,512]{1,0:T(8,128)(2,1)S(1)} %copy-done.3, bf16[1024,512]{1,0:T(8,128)(2,1)S(1)} %copy-done.4, bf16[4,512,512]{2,1,0:T(8,128)(2,1)S(1)} %copy-done), custom_call_target="tpu_custom_call" | custom-call | flops 2147483648 | bytes 8388608 | tf_op jit(solution)/shard_map/pallas_call | solution.py:457
  155.3 1.6 collective-permute-start.23
  157.0 1.2 collective-permute-done.21
  158.3 1.6 collective-permute-start.22
  159.9 5.4 %collective-permute-done.23 = bf16[4,2,9,16,128]{4,3,2,0,1:T(8,128)(2,1)S(1)} collective-permute-done((bf16[4,2,9,16,128]{4,3,2,0,1:T(8,128)(2,1)S(1)}, bf16[4,2,9,16,128]{4,3,2,0,1:T(8,128)(2,1)S(1)}, u32[]{:S(2)}, u32[]{:S(2)}) %collective-permute-start.23) | collective-permute-done | bytes 294944 | tf_op jit(solution)/shard_map/ppermute | solution.py:362
  165.4 1.6 collective-permute-start.24
  167.9 1.6 collective-permute-start.31
  171.2 3.5 %collective-permute-start.26 = (bf16[17,16,128]{2,1,0:T(8,128)(2,1)S(1)}, bf16[17,16,128]{2,1,0:T(8,128)(2,1)S(1)}, u32[]{:S(2)}, u32[]{:S(2)}) collective-permute-start(bf16[17,16,128]{2,1,0:T(8,128)(2,1)S(1)} %get-tuple-element.54), channel_id=1, source_target_pairs={{0,16},{1,17},{2,18},{3,19},{4,20},{5,21},{6,22},{7,23},{8,24},{9,... | collective-permute-start | bytes 208904 | tf_op jit(solution)/shard_map/ppermute | solution.py:362
  175.1 5.4 %collective-permute-done.31 = bf16[4,2,16,16,128]{4,3,2,0,1:T(8,128)(2,1)S(1)} collective-permute-done((bf16[4,2,16,16,128]{4,3,2,0,1:T(8,128)(2,1)S(1)}, bf16[4,2,16,16,128]{4,3,2,0,1:T(8,128)(2,1)S(1)}, u32[]{:S(2)}, u32[]{:S(2)}) %collective-permute-start.31) | collective-permute-done | bytes 524320 | tf_op jit(solution)/shard_map/ppermute | solution.py:362
  181.3 1.4 collective-permute-done.29
  182.8 1.4 collective-permute-start.30
  184.3 3.3 %collective-permute-done.32 = bf16[4,16,16,128]{3,2,1,0:T(8,128)(2,1)S(1)} collective-permute-done((bf16[4,16,16,128]{3,2,1,0:T(8,128)(2,1)S(1)}, bf16[4,16,16,128]{3,2,1,0:T(8,128)(2,1)S(1)}, u32[]{:S(2)}, u32[]{:S(2)}) %collective-permute-start.32) | collective-permute-done | bytes 262176 | tf_op jit(solution)/shard_map/ppermute | solution.py:362
  187.6 1.7 collective-permute-done.30
  190.0 3.5 %collective-permute-start.34 = (bf16[32,16,128]{2,1,0:T(8,128)(2,1)S(1)}, bf16[32,16,128]{2,1,0:T(8,128)(2,1)S(1)}, u32[]{:S(2)}, u32[]{:S(2)}) collective-permute-start(bf16[32,16,128]{2,1,0:T(8,128)(2,1)S(1)} %get-tuple-element.51), channel_id=1, source_target_pairs={{0,16},{1,17},{2,18},{3,19},{4,20},{5,21},{6,22},{7,23},{8,24},{9,... | collective-permute-start | bytes 393224 | tf_op jit(solution)/shard_map/ppermute | solution.py:362
  196.4 4.1 %collective-permute-done.34 = bf16[32,16,128]{2,1,0:T(8,128)(2,1)S(1)} collective-permute-done((bf16[32,16,128]{2,1,0:T(8,128)(2,1)S(1)}, bf16[32,16,128]{2,1,0:T(8,128)(2,1)S(1)}, u32[]{:S(2)}, u32[]{:S(2)}) %collective-permute-start.34) | collective-permute-done | bytes 131104 | tf_op jit(solution)/shard_map/ppermute | solution.py:362
  (123 shorter events, 20.8 us)
Async XLA Ops:
  2.2 12.1 %collective-permute-start = (bf16[17,16,128]{2,1,0:T(8,128)(2,1)S(1)}, bf16[17,16,128]{2,1,0:T(8,128)(2,1)S(1)}, u32[]{:S(2)}, u32[]{:S(2)}) collective-permute-start(bf16[17,16,128]{2,1,0:T(8,128)(2,1)S(1)} %get-tuple-element.59), channel_id=1, source_target_pairs={{0,8},{1,9},{2,10},{3,11},{4,12},{5,13},{6,14},{7,15},{8,0},{9,1},... | collective-permute-start | bytes 208904 | tf_op jit(solution)/shard_map/ppermute | solution.py:362
  5.3 9.0 %collective-permute-start.1 = (bf16[17,16,128]{2,1,0:T(8,128)(2,1)S(1)}, bf16[17,16,128]{2,1,0:T(8,128)(2,1)S(1)}, u32[]{:S(2)}, u32[]{:S(2)}) collective-permute-start(bf16[17,16,128]{2,1,0:T(8,128)(2,1)S(1)} %get-tuple-element.59), channel_id=1, source_target_pairs={{0,16},{1,17},{2,18},{3,19},{4,20},{5,21},{6,22},{7,23},{8,24},{9,... | collective-permute-start | bytes 208904 | tf_op jit(solution)/shard_map/ppermute | solution.py:362
  7.8 6.6 %collective-permute-start.2 = (bf16[17,16,128]{2,1,0:T(8,128)(2,1)S(1)}, bf16[17,16,128]{2,1,0:T(8,128)(2,1)S(1)}, u32[]{:S(2)}, u32[]{:S(2)}) collective-permute-start(bf16[17,16,128]{2,1,0:T(8,128)(2,1)S(1)} %get-tuple-element.59), channel_id=1, source_target_pairs={{0,24},{1,25},{2,26},{3,27},{4,28},{5,29},{6,30},{7,31},{8,16},{9,... | collective-permute-start | bytes 208904 | tf_op jit(solution)/shard_map/ppermute | solution.py:362
  9.8 8.3 %collective-permute-start.10 = (bf16[32,16,128]{2,1,0:T(8,128)(2,1)S(1)}, bf16[32,16,128]{2,1,0:T(8,128)(2,1)S(1)}, u32[]{:S(2)}, u32[]{:S(2)}) collective-permute-start(bf16[32,16,128]{2,1,0:T(8,128)(2,1)S(1)} %bitcast_select_fusion), channel_id=1, source_target_pairs={{0,8},{1,9},{2,10},{3,11},{4,12},{5,13},{6,14},{7,15},{8,0},{9,1},... | collective-permute-start | bytes 393224 | tf_op jit(solution)/shard_map/ppermute | solution.py:362
  10.7 13.4 %collective-permute-start.11 = (bf16[32,16,128]{2,1,0:T(8,128)(2,1)S(1)}, bf16[32,16,128]{2,1,0:T(8,128)(2,1)S(1)}, u32[]{:S(2)}, u32[]{:S(2)}) collective-permute-start(bf16[32,16,128]{2,1,0:T(8,128)(2,1)S(1)} %bitcast_select_fusion), channel_id=1, source_target_pairs={{0,16},{1,17},{2,18},{3,19},{4,20},{5,21},{6,22},{7,23},{8,24},{9,... | collective-permute-start | bytes 393224 | tf_op jit(solution)/shard_map/ppermute | solution.py:362
  14.2 9.9 %collective-permute-start.12 = (bf16[32,16,128]{2,1,0:T(8,128)(2,1)S(1)}, bf16[32,16,128]{2,1,0:T(8,128)(2,1)S(1)}, u32[]{:S(2)}, u32[]{:S(2)}) collective-permute-start(bf16[32,16,128]{2,1,0:T(8,128)(2,1)S(1)} %bitcast_select_fusion), channel_id=1, source_target_pairs={{0,24},{1,25},{2,26},{3,27},{4,28},{5,29},{6,30},{7,31},{8,16},{9,... | collective-permute-start | bytes 393224 | tf_op jit(solution)/shard_map/ppermute | solution.py:362
  14.5 11.3 %collective-permute-start.4 = (bf16[4,17,16,128]{3,2,1,0:T(8,128)(2,1)S(1)}, bf16[4,17,16,128]{3,2,1,0:T(8,128)(2,1)S(1)}, u32[]{:S(2)}, u32[]{:S(2)}) collective-permute-start(bf16[4,17,16,128]{3,2,1,0:T(8,128)(2,1)S(1)} %pad_maximum_fusion.1.refs_0_), channel_id=1, source_target_pairs={{0,2},{1,3},{2,0},{3,1},{4,6},{5,7},{6,4},{7,5},{8,10},{9,11},{10,... | collective-permute-start | bytes 835592 | tf_op jit(solution)/shard_map/ppermute | solution.py:362
  16.1 11.2 %collective-permute-start.6 = (bf16[4,17,16,128]{3,2,1,0:T(8,128)(2,1)S(1)}, bf16[4,17,16,128]{3,2,1,0:T(8,128)(2,1)S(1)}, u32[]{:S(2)}, u32[]{:S(2)}) collective-permute-start(bf16[4,17,16,128]{3,2,1,0:T(8,128)(2,1)S(1)} %pad_maximum_fusion.1.refs_0_), channel_id=1, source_target_pairs={{0,4},{1,5},{2,6},{3,7},{4,0},{5,1},{6,2},{7,3},{8,12},{9,13},{10,... | collective-permute-start | bytes 835592 | tf_op jit(solution)/shard_map/ppermute | solution.py:362
  18.1 10.6 %collective-permute-start.8 = (bf16[4,17,16,128]{3,2,1,0:T(8,128)(2,1)S(1)}, bf16[4,17,16,128]{3,2,1,0:T(8,128)(2,1)}, u32[]{:S(2)}, u32[]{:S(2)}) collective-permute-start(bf16[4,17,16,128]{3,2,1,0:T(8,128)(2,1)S(1)} %pad_maximum_fusion.1.refs_0_), channel_id=1, source_target_pairs={{0,6},{1,7},{2,4},{3,5},{4,2},{5,3},{6,0},{7,1},{8,14},{9,15},{10,... | collective-permute-start | bytes 835592 | tf_op jit(solution)/shard_map/ppermute | solution.py:362
  24.2 16.3 %collective-permute-start.14 = (bf16[4,32,16,128]{3,2,1,0:T(8,128)(2,1)S(1)}, bf16[4,32,16,128]{3,2,1,0:T(8,128)(2,1)S(1)}, u32[]{:S(2)}, u32[]{:S(2)}) collective-permute-start(bf16[4,32,16,128]{3,2,1,0:T(8,128)(2,1)S(1)} %pad_maximum_fusion.refs_0_), channel_id=1, source_target_pairs={{0,2},{1,3},{2,0},{3,1},{4,6},{5,7},{6,4},{7,5},{8,10},{9,11},{10,... | collective-permute-start | bytes 1572872 | tf_op jit(solution)/shard_map/ppermute | solution.py:362
  25.8 14.8 %collective-permute-start.16 = (bf16[4,32,16,128]{3,2,1,0:T(8,128)(2,1)S(1)}, bf16[4,32,16,128]{3,2,1,0:T(8,128)(2,1)S(1)}, u32[]{:S(2)}, u32[]{:S(2)}) collective-permute-start(bf16[4,32,16,128]{3,2,1,0:T(8,128)(2,1)S(1)} %pad_maximum_fusion.refs_0_), channel_id=1, source_target_pairs={{0,4},{1,5},{2,6},{3,7},{4,0},{5,1},{6,2},{7,3},{8,12},{9,13},{10,... | collective-permute-start | bytes 1572872 | tf_op jit(solution)/shard_map/ppermute | solution.py:362
  27.3 23.7 %collective-permute-start.18 = (bf16[4,32,16,128]{3,2,1,0:T(8,128)(2,1)S(1)}, bf16[4,32,16,128]{3,2,1,0:T(8,128)(2,1)S(1)}, u32[]{:S(2)}, u32[]{:S(2)}) collective-permute-start(bf16[4,32,16,128]{3,2,1,0:T(8,128)(2,1)S(1)} %pad_maximum_fusion.refs_0_), channel_id=1, source_target_pairs={{0,6},{1,7},{2,4},{3,5},{4,2},{5,3},{6,0},{7,1},{8,14},{9,15},{10,... | collective-permute-start | bytes 1572872 | tf_op jit(solution)/shard_map/ppermute | solution.py:362
  30.3 21.5 %collective-permute-start.9 = (bf16[4,17,16,128]{3,2,1,0:T(8,128)(2,1)}, bf16[4,17,16,128]{3,2,1,0:T(8,128)(2,1)}, u32[]{:S(2)}, u32[]{:S(2)}) collective-permute-start(bf16[4,17,16,128]{3,2,1,0:T(8,128)(2,1)} %collective-permute-done.8.refs_6_), channel_id=1, source_target_pairs={{0,1},{1,0},{2,3},{3,2},{4,5},{5,4},{6,7},{7,6},{8,9},{9,8},{10,11... | collective-permute-start | bytes 835592 | tf_op jit(solution)/shard_map/ppermute | solution.py:362
  30.7 49.2 %collective-permute-start.13 = (bf16[4,32,16,128]{3,2,1,0:T(8,128)(2,1)S(1)}, bf16[4,32,16,128]{3,2,1,0:T(8,128)(2,1)S(1)}, u32[]{:S(2)}, u32[]{:S(2)}) collective-permute-start(bf16[4,32,16,128]{3,2,1,0:T(8,128)(2,1)S(1)} %pad_maximum_fusion.refs_0_), channel_id=1, source_target_pairs={{0,1},{1,0},{2,3},{3,2},{4,5},{5,4},{6,7},{7,6},{8,9},{9,8},{10,11... | collective-permute-start | bytes 1572872 | tf_op jit(solution)/shard_map/ppermute | solution.py:362
  40.4 39.5 %collective-permute-start.15 = (bf16[4,32,16,128]{3,2,1,0:T(8,128)(2,1)S(1)}, bf16[4,32,16,128]{3,2,1,0:T(8,128)(2,1)S(1)}, u32[]{:S(2)}, u32[]{:S(2)}) collective-permute-start(bf16[4,32,16,128]{3,2,1,0:T(8,128)(2,1)S(1)} %collective-permute-done.14.refs_2_), channel_id=1, source_target_pairs={{0,1},{1,0},{2,3},{3,2},{4,5},{5,4},{6,7},{7,6},{8,9},{9,8},{10,11... | collective-permute-start | bytes 1572872 | tf_op jit(solution)/shard_map/ppermute | solution.py:362
  40.5 39.4 %collective-permute-start.17 = (bf16[4,32,16,128]{3,2,1,0:T(8,128)(2,1)S(1)}, bf16[4,32,16,128]{3,2,1,0:T(8,128)(2,1)}, u32[]{:S(2)}, u32[]{:S(2)}) collective-permute-start(bf16[4,32,16,128]{3,2,1,0:T(8,128)(2,1)S(1)} %collective-permute-done.16.refs_4_), channel_id=1, source_target_pairs={{0,1},{1,0},{2,3},{3,2},{4,5},{5,4},{6,7},{7,6},{8,9},{9,8},{10,11... | collective-permute-start | bytes 1572872 | tf_op jit(solution)/shard_map/ppermute | solution.py:362
  51.0 28.9 %collective-permute-start.19 = (bf16[4,32,16,128]{3,2,1,0:T(8,128)(2,1)S(1)}, bf16[4,32,16,128]{3,2,1,0:T(8,128)(2,1)}, u32[]{:S(2)}, u32[]{:S(2)}) collective-permute-start(bf16[4,32,16,128]{3,2,1,0:T(8,128)(2,1)S(1)} %collective-permute-done.18.refs_6_), channel_id=1, source_target_pairs={{0,1},{1,0},{2,3},{3,2},{4,5},{5,4},{6,7},{7,6},{8,9},{9,8},{10,11... | collective-permute-start | bytes 1572872 | tf_op jit(solution)/shard_map/ppermute | solution.py:362
  144.8 22.2 %collective-permute-start.28 = (bf16[16,32,16,128]{3,2,1,0:T(8,128)(2,1)}, bf16[16,32,16,128]{3,2,1,0:T(8,128)(2,1)S(1)}, u32[]{:S(2)}, u32[]{:S(2)}) collective-permute-start(bf16[16,32,16,128]{3,2,1,0:T(8,128)(2,1)} %get-tuple-element.47), channel_id=1, source_target_pairs={{0,1},{1,0},{2,3},{3,2},{4,5},{5,4},{6,7},{7,6},{8,9},{9,8},{10,11... | collective-permute-start | bytes 6291464 | tf_op jit(solution)/shard_map/ppermute | solution.py:362
  149.5 8.7 %collective-permute-start.21 = (bf16[4,2,8,16,128]{4,3,2,0,1:T(8,128)(2,1)S(1)}, bf16[4,2,8,16,128]{4,3,2,0,1:T(8,128)(2,1)S(1)}, u32[]{:S(2)}, u32[]{:S(2)}) collective-permute-start(bf16[4,2,8,16,128]{4,3,2,0,1:T(8,128)(2,1)S(1)} %fusion.9), channel_id=1, source_target_pairs={{0,4},{1,5},{2,6},{3,7},{4,0},{5,1},{6,2},{7,3},{8,12},{9,13},{10,... | collective-permute-start | bytes 786440 | tf_op jit(solution)/shard_map/ppermute | solution.py:362
  155.3 9.9 %collective-permute-start.23 = (bf16[4,2,9,16,128]{4,3,2,0,1:T(8,128)(2,1)S(1)}, bf16[4,2,9,16,128]{4,3,2,0,1:T(8,128)(2,1)S(1)}, u32[]{:S(2)}, u32[]{:S(2)}) collective-permute-start(bf16[4,2,9,16,128]{4,3,2,0,1:T(8,128)(2,1)S(1)} %fusion.6), channel_id=1, source_target_pairs={{0,2},{1,3},{2,0},{3,1},{4,6},{5,7},{6,4},{7,5},{8,10},{9,11},{10,... | collective-permute-start | bytes 884744 | tf_op jit(solution)/shard_map/ppermute | solution.py:362
  158.3 11.2 %collective-permute-start.22 = (bf16[4,8,16,128]{3,2,1,0:T(8,128)(2,1)S(1)}, bf16[4,8,16,128]{3,2,1,0:T(8,128)(2,1)S(1)}, u32[]{:S(2)}, u32[]{:S(2)}) collective-permute-start(bf16[4,8,16,128]{3,2,1,0:T(8,128)(2,1)S(1)} %fusion.30), channel_id=1, source_target_pairs={{0,2},{1,3},{2,0},{3,1},{4,6},{5,7},{6,4},{7,5},{8,10},{9,11},{10,... | collective-permute-start | bytes 393224 | tf_op jit(solution)/shard_map/ppermute | solution.py:362
  165.4 5.2 %collective-permute-start.24 = (bf16[4,9,16,128]{3,2,1,0:T(8,128)(2,1)S(1)}, bf16[4,9,16,128]{3,2,1,0:T(8,128)(2,1)S(1)}, u32[]{:S(2)}, u32[]{:S(2)}) collective-permute-start(bf16[4,9,16,128]{3,2,1,0:T(8,128)(2,1)S(1)} %fusion.19), channel_id=1, source_target_pairs={{0,4},{1,5},{2,6},{3,7},{4,0},{5,1},{6,2},{7,3},{8,12},{9,13},{10,... | collective-permute-start | bytes 442376 | tf_op jit(solution)/shard_map/ppermute | solution.py:362
  167.9 12.6 %collective-permute-start.31 = (bf16[4,2,16,16,128]{4,3,2,0,1:T(8,128)(2,1)S(1)}, bf16[4,2,16,16,128]{4,3,2,0,1:T(8,128)(2,1)S(1)}, u32[]{:S(2)}, u32[]{:S(2)}) collective-permute-start(bf16[4,2,16,16,128]{4,3,2,0,1:T(8,128)(2,1)S(1)} %fusion.4), channel_id=1, source_target_pairs={{0,2},{1,3},{2,0},{3,1},{4,6},{5,7},{6,4},{7,5},{8,10},{9,11},{10,... | collective-permute-start | bytes 1572872 | tf_op jit(solution)/shard_map/ppermute | solution.py:362
  169.6 13.1 %collective-permute-start.29 = (bf16[4,2,16,16,128]{4,3,2,0,1:T(8,128)(2,1)S(1)}, bf16[4,2,16,16,128]{4,3,2,0,1:T(8,128)(2,1)S(1)}, u32[]{:S(2)}, u32[]{:S(2)}) collective-permute-start(bf16[4,2,16,16,128]{4,3,2,0,1:T(8,128)(2,1)S(1)} %fusion.3), channel_id=1, source_target_pairs={{0,4},{1,5},{2,6},{3,7},{4,0},{5,1},{6,2},{7,3},{8,12},{9,13},{10,... | collective-permute-start | bytes 1572872 | tf_op jit(solution)/shard_map/ppermute | solution.py:362
  170.6 13.6 %collective-permute-start.25 = (bf16[17,16,128]{2,1,0:T(8,128)(2,1)S(1)}, bf16[17,16,128]{2,1,0:T(8,128)(2,1)S(1)}, u32[]{:S(2)}, u32[]{:S(2)}) collective-permute-start(bf16[17,16,128]{2,1,0:T(8,128)(2,1)S(1)} %get-tuple-element.53), channel_id=1, source_target_pairs={{0,8},{1,9},{2,10},{3,11},{4,12},{5,13},{6,14},{7,15},{8,0},{9,1},... | collective-permute-start | bytes 208904 | tf_op jit(solution)/shard_map/ppermute | solution.py:362
  171.2 13.0 %collective-permute-start.26 = (bf16[17,16,128]{2,1,0:T(8,128)(2,1)S(1)}, bf16[17,16,128]{2,1,0:T(8,128)(2,1)S(1)}, u32[]{:S(2)}, u32[]{:S(2)}) collective-permute-start(bf16[17,16,128]{2,1,0:T(8,128)(2,1)S(1)} %get-tuple-element.54), channel_id=1, source_target_pairs={{0,16},{1,17},{2,18},{3,19},{4,20},{5,21},{6,22},{7,23},{8,24},{9,... | collective-permute-start | bytes 208904 | tf_op jit(solution)/shard_map/ppermute | solution.py:362
  174.8 9.4 %collective-permute-start.27 = (bf16[17,16,128]{2,1,0:T(8,128)(2,1)S(1)}, bf16[17,16,128]{2,1,0:T(8,128)(2,1)S(1)}, u32[]{:S(2)}, u32[]{:S(2)}) collective-permute-start(bf16[17,16,128]{2,1,0:T(8,128)(2,1)S(1)} %get-tuple-element.55), channel_id=1, source_target_pairs={{0,24},{1,25},{2,26},{3,27},{4,28},{5,29},{6,30},{7,31},{8,16},{9,... | collective-permute-start | bytes 208904 | tf_op jit(solution)/shard_map/ppermute | solution.py:362
  180.7 6.9 %collective-permute-start.32 = (bf16[4,16,16,128]{3,2,1,0:T(8,128)(2,1)S(1)}, bf16[4,16,16,128]{3,2,1,0:T(8,128)(2,1)S(1)}, u32[]{:S(2)}, u32[]{:S(2)}) collective-permute-start(bf16[4,16,16,128]{3,2,1,0:T(8,128)(2,1)S(1)} %fusion.8), channel_id=1, source_target_pairs={{0,4},{1,5},{2,6},{3,7},{4,0},{5,1},{6,2},{7,3},{8,12},{9,13},{10,... | collective-permute-start | bytes 786440 | tf_op jit(solution)/shard_map/ppermute | solution.py:362
  182.8 6.4 %collective-permute-start.30 = (bf16[4,16,16,128]{3,2,1,0:T(8,128)(2,1)S(1)}, bf16[4,16,16,128]{3,2,1,0:T(8,128)(2,1)S(1)}, u32[]{:S(2)}, u32[]{:S(2)}) collective-permute-start(bf16[4,16,16,128]{3,2,1,0:T(8,128)(2,1)S(1)} %fusion.7), channel_id=1, source_target_pairs={{0,2},{1,3},{2,0},{3,1},{4,6},{5,7},{6,4},{7,5},{8,10},{9,11},{10,... | collective-permute-start | bytes 786440 | tf_op jit(solution)/shard_map/ppermute | solution.py:362
  189.4 7.0 %collective-permute-start.33 = (bf16[32,16,128]{2,1,0:T(8,128)(2,1)S(1)}, bf16[32,16,128]{2,1,0:T(8,128)(2,1)S(1)}, u32[]{:S(2)}, u32[]{:S(2)}) collective-permute-start(bf16[32,16,128]{2,1,0:T(8,128)(2,1)S(1)} %get-tuple-element.50), channel_id=1, source_target_pairs={{0,8},{1,9},{2,10},{3,11},{4,12},{5,13},{6,14},{7,15},{8,0},{9,1},... | collective-permute-start | bytes 393224 | tf_op jit(solution)/shard_map/ppermute | solution.py:362
  190.0 10.5 %collective-permute-start.34 = (bf16[32,16,128]{2,1,0:T(8,128)(2,1)S(1)}, bf16[32,16,128]{2,1,0:T(8,128)(2,1)S(1)}, u32[]{:S(2)}, u32[]{:S(2)}) collective-permute-start(bf16[32,16,128]{2,1,0:T(8,128)(2,1)S(1)} %get-tuple-element.51), channel_id=1, source_target_pairs={{0,16},{1,17},{2,18},{3,19},{4,20},{5,21},{6,22},{7,23},{8,24},{9,... | collective-permute-start | bytes 393224 | tf_op jit(solution)/shard_map/ppermute | solution.py:362
  193.5 6.9 %collective-permute-start.35 = (bf16[32,16,128]{2,1,0:T(8,128)(2,1)S(1)}, bf16[32,16,128]{2,1,0:T(8,128)(2,1)S(1)}, u32[]{:S(2)}, u32[]{:S(2)}) collective-permute-start(bf16[32,16,128]{2,1,0:T(8,128)(2,1)S(1)} %get-tuple-element.52), channel_id=1, source_target_pairs={{0,24},{1,25},{2,26},{3,27},{4,28},{5,29},{6,30},{7,31},{8,16},{9,... | collective-permute-start | bytes 393224 | tf_op jit(solution)/shard_map/ppermute | solution.py:362
  (22 other events, 355.1 us)

commit v3 on v2

v3 whole, which is shorter than its diff:
```python
from functools import partial

import jax
import jax.numpy as jnp
from jax import lax
from jax.experimental import pallas as pl
from jax.experimental.pallas import tpu as pltpu
from jax.sharding import PartitionSpec as P

D = 512
H = 8
HD = 64
FF = 2048
ROWS = 1024
SLOTS = 8
SHORT = 128
MID = 512
LONG = 1024
AXES = ("dp", "fsdp")
PARTS = 32
BF = jnp.bfloat16
F32 = jnp.float32
VMEM = pl.BlockSpec(memory_space=pltpu.VMEM)
SMEM = pl.BlockSpec(memory_space=pltpu.SMEM)


def nn(a, b):
    return lax.dot_general(a, b, (((1,), (0,)), ((), ())), preferred_element_type=F32)


def nt(a, b):
    return lax.dot_general(a, b, (((1,), (1,)), ((), ())), preferred_element_type=F32)


def tn(a, b):
    return lax.dot_general(a, b, (((0,), (0,)), ((), ())), preferred_element_type=F32)


def call(body, outs, ins, scratch, flops, moved, limit, grid=None):
    shapes = [jax.ShapeDtypeStruct(o[0], o[1]) for o in outs]
    return pl.pallas_call(
        body,
        out_shape=shapes,
        grid=grid or (),
        in_specs=ins,
        out_specs=[o[2] if len(o) > 2 else VMEM for o in outs],
        scratch_shapes=[pltpu.VMEM(s, d) for s, d in scratch],
        compiler_params=pltpu.CompilerParams(vmem_limit_bytes=limit << 20),
        cost_estimate=pl.CostEstimate(flops=flops, bytes_accessed=moved, transcendentals=0),
    )


def slot_masks(counts, lengths, keys_out, rows_out):
    lane = lax.broadcasted_iota(jnp.int32, (1, 128), 1)
    slot = lane & 63
    longs, mids, shorts = counts[0, 2], counts[0, 1], counts[0, 0]
    in_long = jnp.minimum(slot, longs)
    in_mid = jnp.clip(slot - longs, 0, mids)
    in_short = jnp.clip(slot - longs - mids, 0, shorts)
    start = in_long * LONG + in_mid * MID + in_short * SHORT
    size = jnp.where(
        slot < longs,
        LONG,
        jnp.where(slot < longs + mids, MID, jnp.where(slot < longs + mids + shorts, SHORT, 0)),
    )
    valid = jnp.zeros((1, 128), jnp.int32)
    for s in range(SLOTS):
        valid = jnp.where(slot == s, lengths[0, s], valid)
    row = lax.broadcasted_iota(jnp.int32, (ROWS, 128), 0)
    member = (row >= start) & (row < start + size)
    usable = (row >= start) & (row < start + valid)
    for parity in range(2):
        here = (slot < SLOTS) & ((lane >= 64) if parity == 0 else (lane < 64))
        rows_out[parity] = jnp.where(here & member, 1.0, 0.0).astype(BF)
        keys_out[parity] = jnp.where(here & jnp.logical_not(usable), -1e30, 0.0).astype(BF)


def half_of(parity, shape):
    lane = lax.broadcasted_iota(jnp.int32, shape, len(shape) - 1)
    return (lane < 64) if parity == 0 else (lane >= 64)


def project_body(n, place, tok, *refs):
    gathered, (q_out, k_out, v_out, x_t, w_out, bias_out) = refs[:8], refs[8:]
    rows_each = D * 4 // n
    tiles = rows_each // 16

    def assemble(z, _):
        for d in range(8):
            o = (8 * z + d) ^ place[0]
            square, row = o // (n // 4), (o % (n // 4)) * rows_each
            for i in range(tiles):
                for j in range(4):
                    w_out[square, pl.ds(pl.multiple_of(row + 16 * i, 16), 16), 128 * j : 128 * j + 128] = (
                        gathered[d][z, 4 * i + j]
                    )
            tail = gathered[d][z, 4 * tiles].astype(F32)
            bias_out[0:1, pl.ds(pl.multiple_of(o * 128, 128), 128)] = tail[0:1]
        return 0

    lax.fori_loop(0, n // 8, assemble, 0)

    def project(r, _):
        at = pl.ds(pl.multiple_of(r * 256, 256), 256)
        x = tok[at, :]
        q = (nn(x, w_out[0]) + bias_out[0:1, 0:D]).astype(BF)
        q_out[at, :] = (q.astype(F32) * 0.125).astype(BF)
        k_out[at, :] = nn(x, w_out[1]).astype(BF)
        v_out[at, :] = (nn(x, w_out[2]) + bias_out[0:1, D : 2 * D]).astype(BF)
        return 0

    lax.fori_loop(0, 4, project, 0)
    x_t[...] = tok[...].T


def attend_body(counts, lengths, q_in, k_in, v_in, ctx_out, lse_out, keys_mask, rows_mask, lse_cols):
    p = pl.program_id(0)

    @pl.when(p == 0)
    def _():
        slot_masks(counts, lengths, keys_mask, rows_mask)
        lse_cols[...] = jnp.zeros_like(lse_cols)

    keys, values = [], []
    for parity in range(2):
        mine = half_of(parity, (ROWS, 128))
        keys.append(jnp.where(mine, k_in[...], keys_mask[parity]))
        values.append(jnp.where(mine, v_in[...], jnp.zeros((ROWS, 128), BF)))
    for r in range(4):
        at = slice(r * 256, r * 256 + 256)
        total = None
        lane = lax.broadcasted_iota(jnp.int32, (256, 128), 1)
        logs = lse_cols[at, :]
        for parity in range(2):
            qa = jnp.where(half_of(parity, (256, 128)), q_in[at, :], rows_mask[parity, at])
            s = nt(qa, keys[parity])
            top = jnp.max(s, axis=1, keepdims=True)
            e = jnp.exp(s - top)
            mass = jnp.sum(e, axis=1, keepdims=True)
            probs = (e * (1.0 / mass)).astype(BF)
            part = nn(probs, values[parity])
            total = part if total is None else total + part
            logs = jnp.where(lane == 2 * p + parity, top + jnp.log(mass), logs)
        ctx_out[at, :] = total.astype(BF)
        lse_cols[at, :] = logs

    @pl.when(p == pl.num_programs(0) - 1)
    def _():
        lse_out[...] = lse_cols[...].T[0:8]


def branch_body(ctx, w, bias, branch_out):
    for r in range(4):
        at = slice(r * 256, r * 256 + 256)
        branch_out[at, :] = nn(ctx[at, :], w[3]) + bias[0:1, 2 * D : 3 * D]


def store_square(odd, keep, send, slot, tile, val, o, width):
    for j in range(width):
        for i in range(4):
            col, top = slice(128 * j, 128 * j + 128), 64 * o + 16 * i
            even, other = val[top : top + 16, col], val[top + 64 : top + 80, col]
            keep[slot, tile + 4 * j + i] = jnp.where(odd, other, even)
            send[slot, tile + 4 * j + i] = jnp.where(odd, even, other)


def feed_body(
    n, place, gates, tok, branch, cot, ctx, w_out, bias, *refs
):
    gathered, refs = refs[:8], refs[8:]
    (layer_out, gm_out, gctx_out, keep_out, send_out, wo_keep, wo_send) = refs[:7]
    (w1, w2, mlow, gbr, gs_all, active_all, gh_all, sums_out) = refs[7:]
    rows_up = D // (n // 2)
    rows_down = FF // (n // 2)
    tiles = rows_down // 16 * 4

    def assemble(z, _):
        for d in range(8):
            o = (8 * z + d) ^ place[0]

            @pl.when(o < n // 2)
            def _():
                for i in range(rows_up // 16):
                    for j in range(16):
                        row = pl.ds(pl.multiple_of(o * rows_up + 16 * i, 16), 16)
                        w1[row, 128 * j : 128 * j + 128] = gathered[d][z, 16 * i + j]

            @pl.when(o >= n // 2)
            def _():
                for i in range(rows_down // 16):
                    for j in range(4):
                        row = pl.ds(pl.multiple_of((o - n // 2) * rows_down + 16 * i, 16), 16)
                        w2[row, 128 * j : 128 * j + 128] = gathered[d][z, 4 * i + j]

        return 0

    lax.fori_loop(0, n // 8, assemble, 0)
    ga, gf = gates[0], gates[1]
    sums_out[...] = jnp.zeros_like(sums_out)
    c1 = 0.7978845608028654
    c2 = 0.044715

    def rows(r, carry):
        attend_sum, feed_sum = carry
        at = pl.ds(pl.multiple_of(r * 256, 256), 256)
        br = branch[at, :]
        middle = tok[at, :].astype(F32) + ga * br
        low = middle.astype(BF)
        mlow[at, :] = low
        ct = cot[at, :].astype(F32)
        gs = (gf * ct).astype(BF)
        gs_all[at, :] = gs
        second = jnp.zeros((256, D), F32) + bias[0:1, 3 * D : 4 * D]
        gmid = ct
        for j in range(4):
            cols = slice(512 * j, 512 * j + 512)
            v = nn(low, w1[:, cols]) + bias[0:1, 4 * D + 512 * j : 4 * D + 512 * j + 512]
            back = nt(gs, w2[cols, :])
            v2 = v * v
            t = jnp.tanh(c1 * v * (1.0 + c2 * v2))
            half = 0.5 * (1.0 + t)
            active = (v * half).astype(BF)
            slope = half + (0.5 * c1) * v * (1.0 - t * t) * (1.0 + (3.0 * c2) * v2)
            gh = (slope * back).astype(BF)
            active_all[at, cols] = active
            gh_all[at, cols] = gh
            sums_out[0:1, 4 * D + 512 * j : 4 * D + 512 * j + 512] += jnp.sum(
                gh.astype(F32), axis=0, keepdims=True
            )
            second = second + nn(active, w2[cols, :])
            gmid = gmid + nt(gh, w1[:, cols])
        layer_out[at, :] = (middle + gf * second).astype(BF)
        gm_out[at, :] = gmid
        gb = (ga * gmid).astype(BF)
        gbr[at, :] = gb
        gctx_out[at, :] = nt(gb, w_out[3]).astype(BF)
        sums_out[0:1, 2 * D : 3 * D] += jnp.sum(gb.astype(F32), axis=0, keepdims=True)
        sums_out[0:1, 3 * D : 4 * D] += jnp.sum(gs.astype(F32), axis=0, keepdims=True)
        attend_sum = attend_sum + jnp.sum(br * gmid, axis=0, keepdims=True)
        feed_sum = feed_sum + jnp.sum(second * ct, axis=0, keepdims=True)
        return attend_sum, feed_sum

    zero = jnp.zeros((1, D), F32)
    attend_sum, feed_sum = lax.fori_loop(0, 4, rows, (zero, zero))
    odd = place[1] == 1

    def store(even_owner, tile, even, other):
        keep_out[even_owner // 2, tile] = jnp.where(odd, other, even)
        send_out[even_owner // 2, tile] = jnp.where(odd, even, other)

    lane = lax.broadcasted_iota(jnp.int32, (1, 128), 1)
    gate = jnp.where(lane == 2 * place[2], jnp.sum(attend_sum), 0.0)
    gate = jnp.where(lane == 2 * place[2] + 1, jnp.sum(feed_sum), gate)
    high = gate.astype(BF).astype(F32)
    rest = gate - high
    mid = rest.astype(BF).astype(F32)
    low = (rest - mid).astype(BF).astype(F32)
    row = lax.broadcasted_iota(jnp.int32, (16, 128), 0)
    base = jnp.where(row == 1, high, jnp.where(row == 2, mid, jnp.where(row == 3, low, 0.0)))
    for o in range(0, n, 2):
        even = jnp.where(row == 0, sums_out[0:1, 128 * o : 128 * o + 128], base)
        other = jnp.where(row == 0, sums_out[0:1, 128 * o + 128 : 128 * o + 256], base)
        store(o, tiles, even, other)
    val = tn(ctx[...], gbr[...])
    for o in range(0, n // 4, 2):
        store_square(odd, wo_keep, wo_send, o // 2, 0, val, o, 4)

    for j in range(4):
        val = tn(mlow[...], gh_all[:, 512 * j : 512 * j + 512])
        for o in range(0, n // 2, 2):
            for i in range(rows_up // 16):
                for jj in range(4):
                    col = slice(128 * jj, 128 * jj + 128)
                    top = o * rows_up + 16 * i
                    store(o, 16 * i + 4 * j + jj, val[top : top + 16, col], val[top + rows_up : top + rows_up + 16, col])
    for j in range(4):
        val = tn(active_all[:, 512 * j : 512 * j + 512], gs_all[...])
        per = 512 // rows_down
        for o in range(0, per, 2):
            for i in range(rows_down // 16):
                for jj in range(4):
                    col = slice(128 * jj, 128 * jj + 128)
                    top = o * rows_down + 16 * i
                    store(
                        n // 2 + j * per + o, 4 * i + jj,
                        val[top : top + 16, col], val[top + rows_down : top + rows_down + 16, col],
                    )


def back_body(first, counts, lengths, place, q_in, k_in, v_in, gctx, lse, x_t, *refs):
    if first:
        before, refs = refs[0], refs[1:]
    dq_out, dk_out, dv_out, keep_out, send_out, *refs = refs
    if first:
        tail_keep, tail_send, *refs = refs
    else:
        sums, *refs = refs
    keys_mask, rows_mask, k_t, dq_t, dk_acc, dv_acc, *refs = refs
    if first:
        (sums,) = refs
    p = pl.program_id(0) + first

    @pl.when(pl.program_id(0) == 0)
    def _():
        slot_masks(counts, lengths, keys_mask, rows_mask)
        sums[...] = before[...] if first else jnp.zeros_like(sums)

    k_t[...] = k_in[...].T
    dk_acc[...] = jnp.zeros_like(dk_acc)
    dv_acc[...] = jnp.zeros_like(dv_acc)
    for parity in range(2):
        mine = half_of(parity, (ROWS, 128))
        ka = jnp.where(mine, k_in[...], keys_mask[parity])
        kt = k_t[64 * parity : 64 * parity + 64, :]
        logs = lse[pl.ds(2 * p + parity, 1), :]
        few = half_of(parity, (256, 128))
        for r in range(4):
            at = slice(r * 256, r * 256 + 256)
            qp = q_in[at, :]
            none = jnp.zeros_like(qp)
            st = nt(ka, jnp.where(few, qp, rows_mask[parity, at]))
            pt = jnp.exp(st - logs[:, at])
            gp = jnp.where(few, gctx[at, :], none)
            dpt = nt(v_in[...], gp)
            delta = jnp.sum(pt * dpt, axis=0, keepdims=True)
            dst = (pt * (dpt - delta)).astype(BF)
            dk_acc[...] += nn(dst, jnp.where(few, qp, none))
            dv_acc[...] += nn(pt.astype(BF), gp)
            dq_t[64 * parity : 64 * parity + 64, at] = nn(kt, dst) * 0.125
    dq = dq_t[...].T.astype(BF)
    dk = dk_acc[...].astype(BF)
    dv = dv_acc[...].astype(BF)
    dq_out[...] = dq
    dk_out[...] = dk
    dv_out[...] = dv
    sums[pl.ds(p, 1), :] = jnp.sum(dq.astype(F32), axis=0, keepdims=True)
    sums[pl.ds(4 + p, 1), :] = jnp.sum(dv.astype(F32), axis=0, keepdims=True)
    odd = place[1] == 1
    val = nn(x_t[...], jnp.concatenate([dq, dk, dv], axis=1))
    for square in range(3):
        for o in range(0, 8, 2):
            store_square(
                odd, keep_out.at[0], send_out.at[0], 4 * square + o // 2, 0,
                val[:, 128 * square : 128 * square + 128], o, 1,
            )
    if first:

        @pl.when(pl.program_id(0) == pl.num_programs(0) - 1)
        def _():
            row = lax.broadcasted_iota(jnp.int32, (16, 128), 0)
            for o in range(0, 8, 2):
                even = jnp.where(row == 0, sums[o : o + 1, :], 0.0)
                other = jnp.where(row == 0, sums[o + 1 : o + 2, :], 0.0)
                tail_keep[o // 2] = jnp.where(odd, other, even)
                tail_send[o // 2] = jnp.where(odd, even, other)


def split_row(tile):
    row = lax.broadcasted_iota(jnp.int32, tile.shape, 0)
    rest = tile[0:1] - tile[0:1].astype(BF).astype(F32)
    return jnp.where(row == 4, rest, tile)


def join_row(tile):
    row = lax.broadcasted_iota(jnp.int32, tile.shape, 0)
    whole = tile[0:1] + tile[4:5]
    return jnp.where(row == 0, whole, jnp.where(row == 4, 0.0, tile))


def feed_xy_body(place, keep, got, wo_keep, wo_got, *outs):
    size = keep.shape[1]
    for t in range(4):
        here = place[3] ^ t
        out = outs[t]
        for z in range(4):
            total = keep[4 * z + here] + got[4 * z + here]
            out[size * z : size * z + size - 1] = total[: size - 1].astype(out.dtype)
            out[size * z + size - 1] = (split_row(total[size - 1]) if t else total[size - 1]).astype(out.dtype)
        out[4 * size :] = (wo_keep[here] + wo_got[here]).astype(out.dtype)


def feed_z_body(place, keep, g1, g2, g3, out0, out1, out2, out3, wo_out):
    size = out0.shape[0]
    for t, out in enumerate((out0, out1, out2, out3)):
        at = pl.ds((place[4] ^ t) * size, size - 1)
        total = keep[at] + g1[at].astype(F32) + g2[at].astype(F32) + g3[at].astype(F32)
        out[: size - 1] = total.astype(out.dtype)
        at = (place[4] ^ t) * size + size - 1
        total = keep[at]
        for g in (g1, g2, g3):
            total = total + join_row(g[at].astype(F32))
        out[size - 1] = (split_row(total) if t else total).astype(out.dtype)
    at = slice(4 * size, 4 * size + 16)
    wo_out[...] = keep[at] + g1[at].astype(F32) + g2[at].astype(F32) + g3[at].astype(F32)


def square_xy_body(place, keep0, got0, keep1, got1, tail_keep, tail_got, *outs):
    for t in range(4):
        here = place[3] ^ t
        out = outs[t]
        for z in range(3):
            for p in range(4):
                keep, got, at = (keep0, got0, 0) if p == 0 else (keep1, got1, p - 1)
                total = keep[at, 4 * z + here] + got[at, 4 * z + here]
                out[16 * z + 4 * p : 16 * z + 4 * p + 4] = total.astype(out.dtype)
        total = tail_keep[here] + tail_got[here]
        out[48] = (split_row(total) if t else total).astype(out.dtype)


def square_z_body(place, keep, g1, g2, g3, wo, out0, out1, out2, out3, whole):
    for z in range(3):
        at = slice(16 * z, 16 * z + 16)
        whole[z, :16] = keep[at] + g1[at].astype(F32) + g2[at].astype(F32) + g3[at].astype(F32)
        whole[z + 1, 16] = jnp.zeros((16, 128), F32)
    whole[3, :16] = wo[...]
    total = keep[48]
    for g in (g1, g2, g3):
        total = total + join_row(g[48].astype(F32))
    whole[0, 16] = total
    for t, out in enumerate((out0, out1, out2, out3)):
        at = place[4] ^ t
        out[:16] = whole[at, :16].astype(out.dtype)
        out[16] = (split_row(whole[at, 16]) if t else whole[at, 16]).astype(out.dtype)


def last_body(keep, g1, g2, g3, out):
    size = keep.shape[0]
    at = slice(0, size - 1)
    out[at] = keep[at] + g1[at].astype(F32) + g2[at].astype(F32) + g3[at].astype(F32)
    total = keep[size - 1]
    for g in (g1, g2, g3):
        total = total + join_row(g[size - 1].astype(F32))
    out[size - 1] = total


def input_body(gm, dq, dk, dv, w, out):
    def rows(r, _):
        at = pl.ds(pl.multiple_of(r * 256, 256), 256)
        out[at, :] = gm[at, :] + nt(dq[at, :], w[0]) + nt(dk[at, :], w[1]) + nt(dv[at, :], w[2])
        return 0

    lax.fori_loop(0, 4, rows, 0)


def to_tiles(flat, rows, cols):
    return flat.reshape(rows // 16, 16, cols // 128, 128).transpose(0, 2, 1, 3).reshape(-1, 16, 128)


def from_tiles(tiles, rows, cols):
    return tiles.reshape(rows // 16, cols // 128, 16, 128).transpose(0, 2, 1, 3).reshape(-1)


def from_columns(tiles, rows):
    return tiles.reshape(-1, rows // 16, 16, 128).transpose(1, 2, 0, 3).reshape(-1)


def swap(x, n, bit):
    return lax.ppermute(x, AXES, [(i, i ^ bit) for i in range(n)])


def small(body, outs, args, scratch=()):
    ins = [SMEM if arg.dtype == jnp.int32 else VMEM for arg in args]
    size = sum(arg.size for arg in args)
    return call(body, outs, ins, scratch, 2 * size, 6 * size, 16)(*args)


def blocks_of(*shape):
    return [(shape + (16, 128), F32)] + [(shape + (16, 128), BF)] * 3


def hop(parts, n, step):
    return [parts[0]] + [swap(part, n, step * t) for t, part in enumerate(parts) if t]


def along_z(own, n):
    return jnp.stack([own] + [swap(own, n, 8 * z) for z in (1, 2, 3)])


def along_xy(stack, n):
    return [stack] + [swap(stack, n, bits) for bits in (2, 4, 6)]


def along_core(chips, n):
    return [part for chip in chips for part in (chip, swap(chip, n, 1))]


def tie(values, after):
    return lax.optimization_barrier((values, after))[0]


def gather(attention, feedforward, biases, n, me):
    rows_each, rows_up, rows_down = 4 * D // n, D // (n // 2), FF // (n // 2)
    tail = jnp.pad(biases[None, None, :], ((0, 0), (0, 15), (0, 0)))
    own_a = jnp.concatenate([to_tiles(attention, rows_each, D), tail], axis=0)
    own_f = jnp.where(
        me < n // 2, to_tiles(feedforward, rows_up, FF), to_tiles(feedforward, rows_down, D)
    )
    stack_a = along_z(own_a, n)
    stack_f = along_z(tie(own_f, stack_a), n)
    return along_core(along_xy(stack_a, n), n), stack_f


def gather_any(attention, feedforward, biases):
    rows_each, rows_up, rows_down = 4 * D // PARTS, D // (PARTS // 2), FF // (PARTS // 2)
    full = lax.all_gather(attention, AXES, axis=0, tiled=True).reshape(PARTS, -1)
    tail = lax.all_gather(biases, AXES, axis=0, tiled=True).reshape(PARTS, 1, 1, 128)
    tail = jnp.pad(tail, ((0, 0), (0, 0), (0, 15), (0, 0)))
    squares = jax.vmap(lambda f: to_tiles(f, rows_each, D))(full)
    full = lax.all_gather(feedforward, AXES, axis=0, tiled=True).reshape(PARTS, -1)
    up = jax.vmap(lambda f: to_tiles(f, rows_up, FF))(full[: PARTS // 2])
    down = jax.vmap(lambda f: to_tiles(f, rows_down, D))(full[PARTS // 2 :])
    pieces = jnp.concatenate([squares, tail], axis=1), jnp.concatenate([up, down])
    return [[p.reshape((4, 8) + p.shape[1:])[:, d] for d in range(8)] for p in pieces]


def local(direct, tokens, cotangent, attention, feedforward, biases, gates, counts, lengths):
    me = lax.axis_index(AXES)
    n = PARTS
    rows_each, rows_up, rows_down = 4 * D // n, D // (n // 2), FF // (n // 2)
    tiles = 4 * rows_each // 16
    ftiles = 4 * rows_down // 16
    if direct:
        ga_all, stack_f = gather(attention, feedforward, biases, n, me)
        place = jnp.stack([me, me % 2, me, (me // 2) % 4, me // 8]).astype(jnp.int32)
    else:
        ga_all, gf_all = gather_any(attention, feedforward, biases)
        place = jnp.zeros((5,), jnp.int32)
    row = (ROWS, D)
    masks = [((2, ROWS, 128), BF), ((2, ROWS, 128), BF)]
    q, k, v, x_t, w, bias = call(
        partial(project_body, n),
        [(row, BF)] * 3 + [((D, ROWS), BF), ((4, D, D), BF), ((1, 8 * D), F32)],
        [SMEM] + [VMEM] * 9, [], 2 << 30, 10 << 20, 48,
    )(place, tokens, *ga_all)
    if direct:
        stack_f, q = lax.optimization_barrier((stack_f, q))
        chips_f = along_xy(stack_f, n)
    pair = pl.BlockSpec((ROWS, 128), lambda i: (0, i))
    ctx, lse = call(
        attend_body,
        [(row, BF, pair), ((8, ROWS), F32, pl.BlockSpec((8, ROWS), lambda i: (0, 0)))],
        [SMEM, SMEM] + [pair] * 3,
        masks + [((ROWS, 128), F32)],
        12 << 30, 4 << 20, 60, (4,),
    )(counts, lengths, q, k, v)
    if direct:
        chips_f, ctx = lax.optimization_barrier((chips_f, ctx))
        gf_all = along_core(chips_f, n)
    (branch,) = call(branch_body, [(row, F32)], [VMEM] * 3, [], 1 << 30, 4 << 20, 32)(ctx, w, bias)
    layer, gm, gctx, ff_keep, ff_send, wo_keep, wo_send = call(
        partial(feed_body, n),
        [(row, BF), (row, F32), (row, BF)] + [((n // 2, ftiles + 1, 16, 128), F32)] * 2
        + [((n // 8, 16, 16, 128), F32)] * 2,
        [SMEM, SMEM] + [VMEM] * 14,
        [((D, FF), BF), ((FF, D), BF), (row, BF), (row, BF), (row, BF), ((ROWS, FF), BF), ((ROWS, FF), BF),
         ((1, 8 * D), F32)],
        14 << 30, 30 << 20, 62,
    )(place, gates, tokens, branch, cotangent, ctx, w, bias, *gf_all)

    def back(first, pairs, q, before):
        cols = pl.BlockSpec((ROWS, 128), lambda i: (0, first + i))
        part = ((ROWS, 128 * pairs), BF, pl.BlockSpec((ROWS, 128), lambda i: (0, i)))
        sent = ((pairs, 12, 4, 16, 128), F32, pl.BlockSpec((1, 12, 4, 16, 128), lambda i: (i, 0, 0, 0, 0)))
        sums = pl.BlockSpec((8, 128), lambda i: (0, 0))
        tail = ((4, 16, 128), F32, pl.BlockSpec((4, 16, 128), lambda i: (0, 0, 0)))
        return call(
            partial(back_body, first),
            [part] * 3 + [sent] * 2 + ([tail] * 2 if first else [((8, 128), F32, sums)]),
            [SMEM] * 3 + [cols] * 4
            + [pl.BlockSpec((8, ROWS), lambda i: (0, 0)), pl.BlockSpec((D, ROWS), lambda i: (0, 0))]
            + ([sums] if first else []),
            masks + [((128, ROWS), BF), ((128, ROWS), F32), ((ROWS, 128), F32), ((ROWS, 128), F32)]
            + ([((8, 128), F32)] if first else []),
            pairs * (5 << 30), 4 << 20, 60, (pairs,),
        )(counts, lengths, place, q, k, v, gctx, lse, x_t, *([before] if first else []))

    if direct:
        got, wo_got = swap(ff_send, n, 1), swap(wo_send, n, 1)
    *part0, keep0, send0, before = back(0, 1, q, None)
    if direct:
        got, wo_got, part0, send0 = lax.optimization_barrier((got, wo_got, part0, send0))
        size = 4 * ftiles + 20
        parts = small(feed_xy_body, blocks_of(size), (place, ff_keep, got, wo_keep, wo_got))
        q, parts = lax.optimization_barrier((q, parts))
        got0 = swap(send0, n, 1)
        ff_got = hop(parts, n, 2)
    part1 = back(1, 3, q, before)
    if direct:
        ff_got, part1 = lax.optimization_barrier((ff_got, part1))
    *part1, keep1, send1, tail_keep, tail_send = part1
    dq, dk, dv = [jnp.concatenate(both, axis=1) for both in zip(part0, part1)]
    if direct:
        got1, tail_got = swap(send1, n, 1), swap(tail_send, n, 1)
        *ff_parts, wo = small(
            feed_z_body, blocks_of(ftiles + 1) + [((16, 16, 128), F32)], (place, *ff_got)
        )
        ff_got = hop(ff_parts, n, 8)
        tail_keep, ff_parts = lax.optimization_barrier((tail_keep, ff_parts))
        parts = small(square_xy_body, blocks_of(49), (place, keep0, got0, keep1, got1, tail_keep, tail_got))
        got = hop(parts, n, 2)
        gm, parts = lax.optimization_barrier((gm, parts))
    (input_grad,) = call(
        input_body, [(row, F32)], [VMEM] * 5, [], 2 << 30, 8 << 20, 32
    )(gm, dq, dk, dv, w)
    if direct:
        got, input_grad, ff_got = lax.optimization_barrier((got, input_grad, ff_got))
        parts = small(square_z_body, blocks_of(17), (place, *got, wo), [((4, 17, 16, 128), F32)])
        got = hop(parts, n, 8)
        ff_got, parts = lax.optimization_barrier((ff_got, parts))
        (ff_shard,) = small(last_body, [((ftiles + 1, 16, 128), F32)], ff_got)
        (att_shard,) = small(last_body, [((17, 16, 128), F32)], got)
        ff_grad = jnp.where(
            me < n // 2, from_tiles(ff_shard[:ftiles], rows_up, FF), from_tiles(ff_shard[:ftiles], rows_down, D)
        )
        att_grad = from_columns(att_shard[:tiles], rows_each)
        tail = ff_shard[ftiles]
        bias_grad = jnp.where(me < 8, att_shard[tiles][0], tail[0])
        gate_grad = jnp.sum((tail[1] + tail[2] + tail[3])[: 2 * n].reshape(n, 2), axis=0)
        return layer, input_grad, att_grad, ff_grad, bias_grad, gate_grad

    def owners(keep, send):
        return jnp.stack([keep, send], axis=1).reshape((-1,) + keep.shape[1:])

    def reduce(flat):
        return lax.psum_scatter(flat.reshape(-1), AXES, scatter_dimension=0, tiled=True)

    both = owners(ff_keep, ff_send)
    up = jax.vmap(lambda t: from_tiles(t, rows_up, FF))(both[: n // 2, :ftiles]).reshape(-1)
    down = jax.vmap(lambda t: from_tiles(t, rows_down, D))(both[n // 2 :, :ftiles]).reshape(-1)
    ff_grad = reduce(jnp.concatenate([up, down]))
    tail = both[0, ftiles]
    gate_grad = lax.psum((tail[1] + tail[2] + tail[3])[:2], AXES)
    bias_grad = jnp.concatenate([owners(tail_keep, tail_send)[:, 0], both[8:, ftiles, 0]])
    keep, send = jnp.concatenate([keep0, keep1]), jnp.concatenate([send0, send1])
    both = jnp.stack([keep, send], axis=2).reshape(4, 24, 4, 16, 128).transpose(1, 0, 2, 3, 4)
    both = jnp.concatenate([both.reshape(24, tiles, 16, 128), owners(wo_keep, wo_send)])
    att_grad = jax.vmap(lambda t: from_columns(t, rows_each))(both)
    return layer, input_grad, reduce(att_grad), ff_grad, reduce(bias_grad), gate_grad


def solution(mesh):
    direct = dict(mesh.shape) == {"dp": 8, "fsdp": 4}
    both = P(AXES)
    rows = P(AXES, None)
    return jax.shard_map(
        partial(local, direct),
        mesh=mesh,
        in_specs=(rows, rows, both, both, both, P(), rows, rows),
        out_specs=(rows, rows, both, both, both, P()),
        check_vma=False,
    )
```

time: 202 us -> 185 us (0.916)
  waiting for transfers between devices: 52.2 us -> 27.3 us
  local copies, waits for them, and re-layouts: 5.9 us -> 15.2 us
  Pallas kernels: 95.2 us -> 103 us
  starting transfers between devices: 40.5 us -> 35.4 us
  other arithmetic: 6.55 us -> 2.89 us
    ppermute x36 -> x37, waiting for transfers between devices: 52.2 us -> 27.3 us  [swap(): return lax.ppermute(x, AXES, [(i, i ^ bit) for i in range(n)])]
    unnamed x36 -> x62, local copies, waits for them, and re-layouts: 1.28 us -> 11.4 us
    pallas_call x3 -> x12, Pallas kernels: 91.5 us -> 99.2 us  [the longest x2 36.4 us: back(): call(partial(back_body, first), [part] * 3 + [sent] * 2 + ([tail] * 2 if...]
    ppermute x36 -> x37, starting transfers between devices: 40.5 us -> 35.4 us  [swap(): return lax.ppermute(x, AXES, [(i, i ^ bit) for i in range(n)])]
    add x13 -> x1, other arithmetic: 3.69 us -> 0.52 us  [local(): tail[1] + tail[2] + tail[3]]
  transfers between devices with their start and end apart: 36 -> 37, of which waited for: 19 -> 13; matrix products, arithmetic and copies ran while one was open for 4% -> 2% of each run, Pallas kernels for 16% -> 35%
where the time goes in v3:
time: 185 us
  Pallas kernels  103 us (56%)
  starting transfers between devices  35.4 us (19%)
  waiting for transfers between devices  27.3 us (15%)
  local copies, waits for them, and re-layouts  15.2 us (8%)
  other arithmetic  2.89 us (2%)
    pallas_call x2, Pallas kernels, back(): call(partial(back_body, first), [part] * 3 + [sent] * 2 + ([tail] * 2 if...  36.4 us
    ppermute x37, starting transfers between devices, swap(): return lax.ppermute(x, AXES, [(i, i ^ bit) for i in range(n)])  35.4 us
    pallas_call x1, Pallas kernels, local(): call(partial(feed_body, n), [(row, BF), (row, F32), (row, BF)] + [((n //...  28.4 us
    ppermute x37, waiting for transfers between devices, swap(): return lax.ppermute(x, AXES, [(i, i ^ bit) for i in range(n)])  27.3 us
    pallas_call x1, Pallas kernels, local(): call(attend_body, [(row, BF, pair), ((8, ROWS), F32, pl.BlockSpec((8, ROW...  20.8 us
    unnamed x62, local copies, waits for them, and re-layouts  11.4 us
    pallas_call x6, Pallas kernels, small(): return call(body, outs, ins, scratch, 2 * size, 6 * size, 16)(*args)  6.91 us
    pallas_call x1, Pallas kernels, local(): call(partial(project_body, n), [(row, BF)] * 3 + [((D, ROWS), BF), ((4, D...  5.96 us
  transfers between devices with their start and end apart: 37, of which 13 were waited for; matrix products, arithmetic and copies ran while one was open for 2% of the time, Pallas kernels for 35%

profile of v3, /device:TPU:0, one launch (start us, length us, event | category | flops | bytes accessed | tf_op | source)
XLA Modules:
  0.0 184.7 jit_solution(9304694676518840186)
XLA Ops:
  2.2 4.1 %collective-permute-start.1 = (bf16[17,16,128]{2,1,0:T(8,128)(2,1)S(1)}, bf16[17,16,128]{2,1,0:T(8,128)(2,1)S(1)}, u32[]{:S(2)}, u32[]{:S(2)}) collective-permute-start(bf16[17,16,128]{2,1,0:T(8,128)(2,1)S(1)} %get-tuple-element.189), channel_id=1, source_target_pairs={{0,16},{1,17},{2,18},{3,19},{4,20},{5,21},{6,22},{7,23},{8,24},{9,... | collective-permute-start | bytes 208904 | tf_op jit(solution)/shard_map/ppermute | solution.py:458
  6.3 1.6 collective-permute-start
  10.6 3.4 %collective-permute-done.2 = bf16[17,16,128]{2,1,0:T(8,128)(2,1)S(1)} collective-permute-done((bf16[17,16,128]{2,1,0:T(8,128)(2,1)S(1)}, bf16[17,16,128]{2,1,0:T(8,128)(2,1)S(1)}, u32[]{:S(2)}, u32[]{:S(2)}) %collective-permute-start.2) | collective-permute-done | bytes 69664 | tf_op jit(solution)/shard_map/ppermute | solution.py:458
  14.0 2.5 %collective-permute-start.11 = (bf16[4,17,16,128]{3,2,1,0:T(8,128)(2,1)S(1)}, bf16[4,17,16,128]{3,2,1,0:T(8,128)(2,1)S(1)}, u32[]{:S(2)}, u32[]{:S(2)}) collective-permute-start(bf16[4,17,16,128]{3,2,1,0:T(8,128)(2,1)S(1)} %pad_maximum_fusion.4.refs_0_), channel_id=1, source_target_pairs={{0,6},{1,7},{2,4},{3,5},{4,2},{5,3},{6,0},{7,1},{8,14},{9,15},{10,... | collective-permute-start | bytes 835592 | tf_op jit(solution)/shard_map/ppermute | solution.py:458
  17.6 1.5 collective-permute-start.5
  19.3 5.1 %collective-permute-done.5 = bf16[32,16,128]{2,1,0:T(8,128)(2,1)S(1)} collective-permute-done((bf16[32,16,128]{2,1,0:T(8,128)(2,1)S(1)}, bf16[32,16,128]{2,1,0:T(8,128)(2,1)S(1)}, u32[]{:S(2)}, u32[]{:S(2)}) %collective-permute-start.5) | collective-permute-done | bytes 131104 | tf_op jit(solution)/shard_map/ppermute | solution.py:458
  25.0 2.8 %collective-permute-done.9.refs_4_ = bf16[4,17,16,128]{3,2,1,0:T(8,128)(2,1)S(1)} collective-permute-done((bf16[4,17,16,128]{3,2,1,0:T(8,128)(2,1)S(1)}, bf16[4,17,16,128]{3,2,1,0:T(8,128)(2,1)S(1)}, u32[]{:S(2)}, u32[]{:S(2)}) %collective-permute-start.9) | collective-permute-done | bytes 278560 | tf_op jit(solution)/shard_map/ppermute | solution.py:458
  28.3 1.9 %collective-permute-done.4 = bf16[32,16,128]{2,1,0:T(8,128)(2,1)S(1)} collective-permute-done((bf16[32,16,128]{2,1,0:T(8,128)(2,1)S(1)}, bf16[32,16,128]{2,1,0:T(8,128)(2,1)S(1)}, u32[]{:S(2)}, u32[]{:S(2)}) %collective-permute-start.4) | collective-permute-done | bytes 131104 | tf_op jit(solution)/shard_map/ppermute | solution.py:458
  30.3 4.9 %collective-permute-done.3 = bf16[32,16,128]{2,1,0:T(8,128)(2,1)S(1)} collective-permute-done((bf16[32,16,128]{2,1,0:T(8,128)(2,1)S(1)}, bf16[32,16,128]{2,1,0:T(8,128)(2,1)S(1)}, u32[]{:S(2)}, u32[]{:S(2)}) %collective-permute-start.3) | collective-permute-done | bytes 131104 | tf_op jit(solution)/shard_map/ppermute | solution.py:458
  35.3 6.0 %shard_map.127 = (bf16[1024,512]{1,0:T(8,128)(2,1)S(1)}, bf16[1024,512]{1,0:T(8,128)(2,1)S(1)}, bf16[1024,512]{1,0:T(8,128)(2,1)S(1)}, bf16[512,1024]{1,0:T(8,12...) custom-call(s32[5]{0:T(128)S(1)} %stack.50.place, bf16[1024,512]{1,0:T(8,128)(2,1)} %tok.3, ...), custom_call_target="tpu_custom_call" | custom-call | flops 2147483648 | bytes 10485760 | tf_op jit(solution)/shard_map/pallas_call | solution.py:530
  44.2 2.4 %collective-permute-start.15 = (bf16[4,32,16,128]{3,2,1,0:T(8,128)(2,1)S(1)}, bf16[4,32,16,128]{3,2,1,0:T(8,128)(2,1)S(1)}, u32[]{:S(2)}, u32[]{:S(2)}) collective-permute-start(bf16[4,32,16,128]{3,2,1,0:T(8,128)(2,1)S(1)} %pad_maximum_fusion.3.refs_0_), channel_id=1, source_target_pairs={{0,6},{1,7},{2,4},{3,5},{4,2},{5,3},{6,0},{7,1},{8,14},{9,15},{10,... | collective-permute-start | bytes 1572872 | tf_op jit(solution)/shard_map/ppermute | solution.py:458
  47.7 20.8 %shard_map.128 = (bf16[1024,512]{1,0:T(8,128)(2,1)}, f32[8,1024]{1,0:T(8,128)}) custom-call(s32[1,3]{1,0:T(1,128)} %counts.5, s32[1,8]{1,0:T(1,128)} %lengths.5, bf16[1024,512]{1,0:T(8,128)(2,1)} %copy-done.16, bf16[1024,512]{1,0:T(8,128)(2,1)} %copy-done.17, bf16[1024,512]{1,0:T(8,128)(2,1)} %copy-done.18), custom_call_target="tpu_custom_call" | custom-call | flops 12884901888 | bytes 4194304 | tf_op jit(solution)/shard_map/pallas_call | solution.py:539
  69.8 1.2 copy-done.6
  71.7 1.3 copy-done.3
  74.8 28.4 %shard_map.130 = (bf16[1024,512]{1,0:T(8,128)(2,1)}, f32[1024,512]{1,0:T(8,128)}, bf16[1024,512]{1,0:T(8,128)(2,1)}, f32[16,33,16,128]{3,2,1,0:T(8,128)}, f32[16...) custom-call(s32[5]{0:T(128)} %copy-done.13, f32[2]{0:T(128)} %gates.1, ...), custom_call_target="tpu_custom_call" | custom-call | flops 15032385536 | bytes 31457280 | tf_op jit(solution)/shard_map/pallas_call | solution.py:550
  103.7 10.2 %shard_map.131 = (bf16[1024,128]{1,0:T(8,128)(2,1)}, bf16[1024,128]{1,0:T(8,128)(2,1)}, bf16[1024,128]{1,0:T(8,128)(2,1)}, f32[1,12,4,16,128]{4,3,2,1,0:T(8,128)...) custom-call(s32[1,3]{1,0:T(1,128)} %counts.5, s32[1,8]{1,0:T(1,128)} %lengths.5, s32[5]{0:T(128)} %copy-done.13, ...), custom_call_target="tpu_custom_call" | custom-call | flops 5368709120 | bytes 4194304 | tf_op jit(solution)/shard_map/pallas_call | solution.py:566
  114.0 2.2 %copy-done.2 = f32[16,33,16,128]{3,2,1,0:T(8,128)S(1)} copy-done((f32[16,33,16,128]{3,2,1,0:T(8,128)S(1)}, f32[16,33,16,128]{3,2,1,0:T(8,128)}, u32[]{:S(2)}) %copy-start.2) | copy-done | bytes 4325400
  116.2 3.8 %shard_map.132 = (f32[148,16,128]{2,1,0:T(8,128)S(1)}, bf16[148,16,128]{2,1,0:T(8,128)(2,1)}, bf16[148,16,128]{2,1,0:T(8,128)(2,1)}, bf16[148,16,128]{2,1,0:T(8,128)(2,1)}) custom-call(s32[5]{0:T(128)S(1)} %copy-done.14, f32[16,33,16,128]{3,2,1,0:T(8,128)S(1)} %copy-done.2, f32[16,33,16,128]{3,2,1,0:T(8,128)} %collective-permute-done.20.got, ...), custom_call_target="tpu_custom_call" | custom-call | flops 4849674 | bytes 14549022 | tf_op jit(solution)/shard_map/pallas_call | solution.py:464
  120.0 1.5 collective-permute-start.23
  121.5 1.5 collective-permute-start.24
  123.5 26.1 %shard_map.133 = (bf16[1024,384]{1,0:T(8,128)(2,1)}, bf16[1024,384]{1,0:T(8,128)(2,1)}, bf16[1024,384]{1,0:T(8,128)(2,1)}, f32[3,12,4,16,128]{4,3,2,1,0:T(8,128)...) custom-call(s32[1,3]{1,0:T(1,128)} %counts.5, s32[1,8]{1,0:T(1,128)} %lengths.5, ...), custom_call_target="tpu_custom_call" | custom-call | flops 16106127360 | bytes 4194304 | tf_op jit(solution)/shard_map/pallas_call | solution.py:566
  152.1 1.5 shard_map.134
  154.5 3.6 %collective-permute-start.32 = (bf16[33,16,128]{2,1,0:T(8,128)(2,1)S(1)}, bf16[33,16,128]{2,1,0:T(8,128)(2,1)S(1)}, u32[]{:S(2)}, u32[]{:S(2)}) collective-permute-start(bf16[33,16,128]{2,1,0:T(8,128)(2,1)S(1)} %get-tuple-element.152), channel_id=1, source_target_pairs={{0,16},{1,17},{2,18},{3,19},{4,20},{5,21},{6,22},{7,23},{8,24},{9,... | collective-permute-start | bytes 405512 | tf_op jit(solution)/shard_map/ppermute | solution.py:458
  160.4 1.4 collective-permute-start.28
  161.8 1.5 collective-permute-start.29
  163.3 1.4 collective-permute-start.30
  164.8 3.7 %shard_map.136 = f32[1024,512]{1,0:T(8,128)} custom-call(f32[1024,512]{1,0:T(8,128)S(1)} %copy-done.4, bf16[1024,512]{1,0:T(8,128)(2,1)S(1)} %get-tuple-element.190.dq, bf16[1024,512]{1,0:T(8,128)(2,1)S(1)} %get-tuple-element.191.dk, bf16[1024,512]{1,0:T(8,128)(2,1)S(1)} %pad_maximum_fusion.2.dv, bf16[4,512,512]{2,1,0:T(8,128)(2,1)S(1)} %copy-done.1), custom_call_target="tpu_custom_call" | custom-call | flops 2147483648 | bytes 8388608 | tf_op jit(solution)/shard_map/pallas_call | solution.py:602
  169.7 3.0 %collective-permute-done.30.g3 = bf16[49,16,128]{2,1,0:T(8,128)(2,1)S(1)} collective-permute-done((bf16[49,16,128]{2,1,0:T(8,128)(2,1)S(1)}, bf16[49,16,128]{2,1,0:T(8,128)(2,1)S(1)}, u32[]{:S(2)}, u32[]{:S(2)}) %collective-permute-start.30) | collective-permute-done | bytes 200736 | tf_op jit(solution)/shard_map/ppermute | solution.py:458
  174.0 2.6 %collective-permute-start.35 = (bf16[17,16,128]{2,1,0:T(8,128)(2,1)S(1)}, bf16[17,16,128]{2,1,0:T(8,128)(2,1)S(1)}, u32[]{:S(2)}, u32[]{:S(2)}) collective-permute-start(bf16[17,16,128]{2,1,0:T(8,128)(2,1)S(1)} %get-tuple-element.176), channel_id=1, source_target_pairs={{0,16},{1,17},{2,18},{3,19},{4,20},{5,21},{6,22},{7,23},{8,24},{9,... | collective-permute-start | bytes 208904 | tf_op jit(solution)/shard_map/ppermute | solution.py:458
  176.6 1.3 collective-permute-start.36
  179.0 1.8 collective-permute-done.35.g2
  180.7 2.0 %collective-permute-done.36.g3 = bf16[17,16,128]{2,1,0:T(8,128)(2,1)S(1)} collective-permute-done((bf16[17,16,128]{2,1,0:T(8,128)(2,1)S(1)}, bf16[17,16,128]{2,1,0:T(8,128)(2,1)S(1)}, u32[]{:S(2)}, u32[]{:S(2)}) %collective-permute-start.36) | collective-permute-done | bytes 69664 | tf_op jit(solution)/shard_map/ppermute | solution.py:458
  (137 shorter events, 26.5 us)
Async XLA Ops:
  2.2 7.6 %collective-permute-start.1 = (bf16[17,16,128]{2,1,0:T(8,128)(2,1)S(1)}, bf16[17,16,128]{2,1,0:T(8,128)(2,1)S(1)}, u32[]{:S(2)}, u32[]{:S(2)}) collective-permute-start(bf16[17,16,128]{2,1,0:T(8,128)(2,1)S(1)} %get-tuple-element.189), channel_id=1, source_target_pairs={{0,16},{1,17},{2,18},{3,19},{4,20},{5,21},{6,22},{7,23},{8,24},{9,... | collective-permute-start | bytes 208904 | tf_op jit(solution)/shard_map/ppermute | solution.py:458
  7.8 6.1 %collective-permute-start.2 = (bf16[17,16,128]{2,1,0:T(8,128)(2,1)S(1)}, bf16[17,16,128]{2,1,0:T(8,128)(2,1)S(1)}, u32[]{:S(2)}, u32[]{:S(2)}) collective-permute-start(bf16[17,16,128]{2,1,0:T(8,128)(2,1)S(1)} %get-tuple-element.189), channel_id=1, source_target_pairs={{0,24},{1,25},{2,26},{3,27},{4,28},{5,29},{6,30},{7,31},{8,16},{9,... | collective-permute-start | bytes 208904 | tf_op jit(solution)/shard_map/ppermute | solution.py:458
  14.0 10.6 %collective-permute-start.11 = (bf16[4,17,16,128]{3,2,1,0:T(8,128)(2,1)S(1)}, bf16[4,17,16,128]{3,2,1,0:T(8,128)(2,1)S(1)}, u32[]{:S(2)}, u32[]{:S(2)}) collective-permute-start(bf16[4,17,16,128]{3,2,1,0:T(8,128)(2,1)S(1)} %pad_maximum_fusion.4.refs_0_), channel_id=1, source_target_pairs={{0,6},{1,7},{2,4},{3,5},{4,2},{5,3},{6,0},{7,1},{8,14},{9,15},{10,... | collective-permute-start | bytes 835592 | tf_op jit(solution)/shard_map/ppermute | solution.py:458
  16.5 11.3 %collective-permute-start.9 = (bf16[4,17,16,128]{3,2,1,0:T(8,128)(2,1)S(1)}, bf16[4,17,16,128]{3,2,1,0:T(8,128)(2,1)S(1)}, u32[]{:S(2)}, u32[]{:S(2)}) collective-permute-start(bf16[4,17,16,128]{3,2,1,0:T(8,128)(2,1)S(1)} %pad_maximum_fusion.4.refs_0_), channel_id=1, source_target_pairs={{0,4},{1,5},{2,6},{3,7},{4,0},{5,1},{6,2},{7,3},{8,12},{9,13},{10,... | collective-permute-start | bytes 835592 | tf_op jit(solution)/shard_map/ppermute | solution.py:458
  17.0 10.8 %collective-permute-start.7 = (bf16[4,17,16,128]{3,2,1,0:T(8,128)(2,1)S(1)}, bf16[4,17,16,128]{3,2,1,0:T(8,128)(2,1)S(1)}, u32[]{:S(2)}, u32[]{:S(2)}) collective-permute-start(bf16[4,17,16,128]{3,2,1,0:T(8,128)(2,1)S(1)} %pad_maximum_fusion.4.refs_0_), channel_id=1, source_target_pairs={{0,2},{1,3},{2,0},{3,1},{4,6},{5,7},{6,4},{7,5},{8,10},{9,11},{10,... | collective-permute-start | bytes 835592 | tf_op jit(solution)/shard_map/ppermute | solution.py:458
  17.6 6.9 %collective-permute-start.5 = (bf16[32,16,128]{2,1,0:T(8,128)(2,1)S(1)}, bf16[32,16,128]{2,1,0:T(8,128)(2,1)S(1)}, u32[]{:S(2)}, u32[]{:S(2)}) collective-permute-start(bf16[32,16,128]{2,1,0:T(8,128)(2,1)S(1)} %bitcast_select_fusion), channel_id=1, source_target_pairs={{0,24},{1,25},{2,26},{3,27},{4,28},{5,29},{6,30},{7,31},{8,16},{9,... | collective-permute-start | bytes 393224 | tf_op jit(solution)/shard_map/ppermute | solution.py:458
  19.1 11.1 %collective-permute-start.4 = (bf16[32,16,128]{2,1,0:T(8,128)(2,1)S(1)}, bf16[32,16,128]{2,1,0:T(8,128)(2,1)S(1)}, u32[]{:S(2)}, u32[]{:S(2)}) collective-permute-start(bf16[32,16,128]{2,1,0:T(8,128)(2,1)S(1)} %bitcast_select_fusion), channel_id=1, source_target_pairs={{0,16},{1,17},{2,18},{3,19},{4,20},{5,21},{6,22},{7,23},{8,24},{9,... | collective-permute-start | bytes 393224 | tf_op jit(solution)/shard_map/ppermute | solution.py:458
  24.5 10.8 %collective-permute-start.6 = (bf16[4,17,16,128]{3,2,1,0:T(8,128)(2,1)S(1)}, bf16[4,17,16,128]{3,2,1,0:T(8,128)(2,1)S(1)}, u32[]{:S(2)}, u32[]{:S(2)}) collective-permute-start(bf16[4,17,16,128]{3,2,1,0:T(8,128)(2,1)S(1)} %pad_maximum_fusion.4.refs_0_), channel_id=1, source_target_pairs={{0,1},{1,0},{2,3},{3,2},{4,5},{5,4},{6,7},{7,6},{8,9},{9,8},{10,11... | collective-permute-start | bytes 835592 | tf_op jit(solution)/shard_map/ppermute | solution.py:458
  24.6 10.7 %collective-permute-start.12 = (bf16[4,17,16,128]{3,2,1,0:T(8,128)(2,1)S(1)}, bf16[4,17,16,128]{3,2,1,0:T(8,128)(2,1)S(1)}, u32[]{:S(2)}, u32[]{:S(2)}) collective-permute-start(bf16[4,17,16,128]{3,2,1,0:T(8,128)(2,1)S(1)} %collective-permute-done.11.refs_6_), channel_id=1, source_target_pairs={{0,1},{1,0},{2,3},{3,2},{4,5},{5,4},{6,7},{7,6},{8,9},{9,8},{10,11... | collective-permute-start | bytes 835592 | tf_op jit(solution)/shard_map/ppermute | solution.py:458
  27.8 7.5 %collective-permute-start.10 = (bf16[4,17,16,128]{3,2,1,0:T(8,128)(2,1)S(1)}, bf16[4,17,16,128]{3,2,1,0:T(8,128)(2,1)S(1)}, u32[]{:S(2)}, u32[]{:S(2)}) collective-permute-start(bf16[4,17,16,128]{3,2,1,0:T(8,128)(2,1)S(1)} %collective-permute-done.9.refs_4_), channel_id=1, source_target_pairs={{0,1},{1,0},{2,3},{3,2},{4,5},{5,4},{6,7},{7,6},{8,9},{9,8},{10,11... | collective-permute-start | bytes 835592 | tf_op jit(solution)/shard_map/ppermute | solution.py:458
  27.8 7.5 %collective-permute-start.8 = (bf16[4,17,16,128]{3,2,1,0:T(8,128)(2,1)S(1)}, bf16[4,17,16,128]{3,2,1,0:T(8,128)(2,1)S(1)}, u32[]{:S(2)}, u32[]{:S(2)}) collective-permute-start(bf16[4,17,16,128]{3,2,1,0:T(8,128)(2,1)S(1)} %collective-permute-done.7.refs_2_), channel_id=1, source_target_pairs={{0,1},{1,0},{2,3},{3,2},{4,5},{5,4},{6,7},{7,6},{8,9},{9,8},{10,11... | collective-permute-start | bytes 835592 | tf_op jit(solution)/shard_map/ppermute | solution.py:458
  44.2 24.3 %collective-permute-start.15 = (bf16[4,32,16,128]{3,2,1,0:T(8,128)(2,1)S(1)}, bf16[4,32,16,128]{3,2,1,0:T(8,128)(2,1)S(1)}, u32[]{:S(2)}, u32[]{:S(2)}) collective-permute-start(bf16[4,32,16,128]{3,2,1,0:T(8,128)(2,1)S(1)} %pad_maximum_fusion.3.refs_0_), channel_id=1, source_target_pairs={{0,6},{1,7},{2,4},{3,5},{4,2},{5,3},{6,0},{7,1},{8,14},{9,15},{10,... | collective-permute-start | bytes 1572872 | tf_op jit(solution)/shard_map/ppermute | solution.py:458
  46.7 22.0 %collective-permute-start.14 = (bf16[4,32,16,128]{3,2,1,0:T(8,128)(2,1)S(1)}, bf16[4,32,16,128]{3,2,1,0:T(8,128)(2,1)S(1)}, u32[]{:S(2)}, u32[]{:S(2)}) collective-permute-start(bf16[4,32,16,128]{3,2,1,0:T(8,128)(2,1)S(1)} %pad_maximum_fusion.3.refs_0_), channel_id=1, source_target_pairs={{0,4},{1,5},{2,6},{3,7},{4,0},{5,1},{6,2},{7,3},{8,12},{9,13},{10,... | collective-permute-start | bytes 1572872 | tf_op jit(solution)/shard_map/ppermute | solution.py:458
  47.2 21.4 %collective-permute-start.13 = (bf16[4,32,16,128]{3,2,1,0:T(8,128)(2,1)S(1)}, bf16[4,32,16,128]{3,2,1,0:T(8,128)(2,1)}, u32[]{:S(2)}, u32[]{:S(2)}) collective-permute-start(bf16[4,32,16,128]{3,2,1,0:T(8,128)(2,1)S(1)} %pad_maximum_fusion.3.refs_0_), channel_id=1, source_target_pairs={{0,2},{1,3},{2,0},{3,1},{4,6},{5,7},{6,4},{7,5},{8,10},{9,11},{10,... | collective-permute-start | bytes 1572872 | tf_op jit(solution)/shard_map/ppermute | solution.py:458
  69.3 5.5 %collective-permute-start.19 = (bf16[4,32,16,128]{3,2,1,0:T(8,128)(2,1)S(1)}, bf16[4,32,16,128]{3,2,1,0:T(8,128)(2,1)}, u32[]{:S(2)}, u32[]{:S(2)}) collective-permute-start(bf16[4,32,16,128]{3,2,1,0:T(8,128)(2,1)S(1)} %collective-permute-done.15.refs_6_), channel_id=1, source_target_pairs={{0,1},{1,0},{2,3},{3,2},{4,5},{5,4},{6,7},{7,6},{8,9},{9,8},{10,11... | collective-permute-start | bytes 1572872 | tf_op jit(solution)/shard_map/ppermute | solution.py:458
  103.2 10.8 %collective-permute-start.20 = (f32[16,33,16,128]{3,2,1,0:T(8,128)}, f32[16,33,16,128]{3,2,1,0:T(8,128)}, u32[]{:S(2)}, u32[]{:S(2)}) collective-permute-start(f32[16,33,16,128]{3,2,1,0:T(8,128)} %get-tuple-element.115), channel_id=1, source_target_pairs={{0,1},{1,0},{2,3},{3,2},{4,5},{5,4},{6,7},{7,6},{8,9},{9,8},{10,11... | collective-permute-start | bytes 12976136 | tf_op jit(solution)/shard_map/ppermute | solution.py:458
  103.3 10.7 %collective-permute-start.21 = (f32[4,16,16,128]{3,2,1,0:T(8,128)}, f32[4,16,16,128]{3,2,1,0:T(8,128)S(1)}, u32[]{:S(2)}, u32[]{:S(2)}) collective-permute-start(f32[4,16,16,128]{3,2,1,0:T(8,128)} %get-tuple-element.116), channel_id=1, source_target_pairs={{0,1},{1,0},{2,3},{3,2},{4,5},{5,4},{6,7},{7,6},{8,9},{9,8},{10,11... | collective-permute-start | bytes 1572872 | tf_op jit(solution)/shard_map/ppermute | solution.py:458
  120.0 29.6 %collective-permute-start.23 = (bf16[148,16,128]{2,1,0:T(8,128)(2,1)}, bf16[148,16,128]{2,1,0:T(8,128)(2,1)S(1)}, u32[]{:S(2)}, u32[]{:S(2)}) collective-permute-start(bf16[148,16,128]{2,1,0:T(8,128)(2,1)} %get-tuple-element.131), channel_id=1, source_target_pairs={{0,2},{1,3},{2,0},{3,1},{4,6},{5,7},{6,4},{7,5},{8,10},{9,11},{10,... | collective-permute-start | bytes 1818632 | tf_op jit(solution)/shard_map/ppermute | solution.py:458
  121.5 28.2 %collective-permute-start.24 = (bf16[148,16,128]{2,1,0:T(8,128)(2,1)}, bf16[148,16,128]{2,1,0:T(8,128)(2,1)S(1)}, u32[]{:S(2)}, u32[]{:S(2)}) collective-permute-start(bf16[148,16,128]{2,1,0:T(8,128)(2,1)} %get-tuple-element.132), channel_id=1, source_target_pairs={{0,4},{1,5},{2,6},{3,7},{4,0},{5,1},{6,2},{7,3},{8,12},{9,13},{10,... | collective-permute-start | bytes 1818632 | tf_op jit(solution)/shard_map/ppermute | solution.py:458
  123.0 27.5 %collective-permute-start.25 = (bf16[148,16,128]{2,1,0:T(8,128)(2,1)}, bf16[148,16,128]{2,1,0:T(8,128)(2,1)}, u32[]{:S(2)}, u32[]{:S(2)}) collective-permute-start(bf16[148,16,128]{2,1,0:T(8,128)(2,1)} %get-tuple-element.133), channel_id=1, source_target_pairs={{0,6},{1,7},{2,4},{3,5},{4,2},{5,3},{6,0},{7,1},{8,14},{9,15},{10,... | collective-permute-start | bytes 1818632 | tf_op jit(solution)/shard_map/ppermute | solution.py:458
  150.5 9.0 %collective-permute-start.26 = (f32[3,12,4,16,128]{4,3,2,1,0:T(8,128)}, f32[3,12,4,16,128]{4,3,2,1,0:T(8,128)S(1)}, u32[]{:S(2)}, u32[]{:S(2)}) collective-permute-start(f32[3,12,4,16,128]{4,3,2,1,0:T(8,128)} %get-tuple-element.144), channel_id=1, source_target_pairs={{0,1},{1,0},{2,3},{3,2},{4,5},{5,4},{6,7},{7,6},{8,9},{9,8},{10,11... | collective-permute-start | bytes 3538952 | tf_op jit(solution)/shard_map/ppermute | solution.py:458
  150.5 8.0 %collective-permute-start.22 = (f32[1,12,4,16,128]{4,3,2,1,0:T(8,128)}, f32[1,12,4,16,128]{4,3,2,1,0:T(8,128)S(1)}, u32[]{:S(2)}, u32[]{:S(2)}) collective-permute-start(f32[1,12,4,16,128]{4,3,2,1,0:T(8,128)} %get-tuple-element.121), channel_id=1, source_target_pairs={{0,1},{1,0},{2,3},{3,2},{4,5},{5,4},{6,7},{7,6},{8,9},{9,8},{10,11... | collective-permute-start | bytes 1179656 | tf_op jit(solution)/shard_map/ppermute | solution.py:458
  151.0 8.5 %collective-permute-start.27 = (f32[4,16,128]{2,1,0:T(8,128)}, f32[4,16,128]{2,1,0:T(8,128)S(1)}, u32[]{:S(2)}, u32[]{:S(2)}) collective-permute-start(f32[4,16,128]{2,1,0:T(8,128)} %get-tuple-element.155), channel_id=1, source_target_pairs={{0,1},{1,0},{2,3},{3,2},{4,5},{5,4},{6,7},{7,6},{8,9},{9,8},{10,11... | collective-permute-start | bytes 98312 | tf_op jit(solution)/shard_map/ppermute | solution.py:458
  153.6 9.7 %collective-permute-start.31 = (bf16[33,16,128]{2,1,0:T(8,128)(2,1)S(1)}, bf16[33,16,128]{2,1,0:T(8,128)(2,1)S(1)}, u32[]{:S(2)}, u32[]{:S(2)}) collective-permute-start(bf16[33,16,128]{2,1,0:T(8,128)(2,1)S(1)} %get-tuple-element.151), channel_id=1, source_target_pairs={{0,8},{1,9},{2,10},{3,11},{4,12},{5,13},{6,14},{7,15},{8,0},{9,1},... | collective-permute-start | bytes 405512 | tf_op jit(solution)/shard_map/ppermute | solution.py:458
  154.5 14.0 %collective-permute-start.32 = (bf16[33,16,128]{2,1,0:T(8,128)(2,1)S(1)}, bf16[33,16,128]{2,1,0:T(8,128)(2,1)S(1)}, u32[]{:S(2)}, u32[]{:S(2)}) collective-permute-start(bf16[33,16,128]{2,1,0:T(8,128)(2,1)S(1)} %get-tuple-element.152), channel_id=1, source_target_pairs={{0,16},{1,17},{2,18},{3,19},{4,20},{5,21},{6,22},{7,23},{8,24},{9,... | collective-permute-start | bytes 405512 | tf_op jit(solution)/shard_map/ppermute | solution.py:458
  158.5 10.0 %collective-permute-start.33 = (bf16[33,16,128]{2,1,0:T(8,128)(2,1)S(1)}, bf16[33,16,128]{2,1,0:T(8,128)(2,1)S(1)}, u32[]{:S(2)}, u32[]{:S(2)}) collective-permute-start(bf16[33,16,128]{2,1,0:T(8,128)(2,1)S(1)} %get-tuple-element.153), channel_id=1, source_target_pairs={{0,24},{1,25},{2,26},{3,27},{4,28},{5,29},{6,30},{7,31},{8,16},{9,... | collective-permute-start | bytes 405512 | tf_op jit(solution)/shard_map/ppermute | solution.py:458
  160.4 8.1 %collective-permute-start.28 = (bf16[49,16,128]{2,1,0:T(8,128)(2,1)S(1)}, bf16[49,16,128]{2,1,0:T(8,128)(2,1)S(1)}, u32[]{:S(2)}, u32[]{:S(2)}) collective-permute-start(bf16[49,16,128]{2,1,0:T(8,128)(2,1)S(1)} %get-tuple-element.157), channel_id=1, source_target_pairs={{0,2},{1,3},{2,0},{3,1},{4,6},{5,7},{6,4},{7,5},{8,10},{9,11},{10,... | collective-permute-start | bytes 602120 | tf_op jit(solution)/shard_map/ppermute | solution.py:458
  161.8 7.9 %collective-permute-start.29 = (bf16[49,16,128]{2,1,0:T(8,128)(2,1)S(1)}, bf16[49,16,128]{2,1,0:T(8,128)(2,1)S(1)}, u32[]{:S(2)}, u32[]{:S(2)}) collective-permute-start(bf16[49,16,128]{2,1,0:T(8,128)(2,1)S(1)} %get-tuple-element.158), channel_id=1, source_target_pairs={{0,4},{1,5},{2,6},{3,7},{4,0},{5,1},{6,2},{7,3},{8,12},{9,13},{10,... | collective-permute-start | bytes 602120 | tf_op jit(solution)/shard_map/ppermute | solution.py:458
  163.3 9.4 %collective-permute-start.30 = (bf16[49,16,128]{2,1,0:T(8,128)(2,1)S(1)}, bf16[49,16,128]{2,1,0:T(8,128)(2,1)S(1)}, u32[]{:S(2)}, u32[]{:S(2)}) collective-permute-start(bf16[49,16,128]{2,1,0:T(8,128)(2,1)S(1)} %get-tuple-element.159), channel_id=1, source_target_pairs={{0,6},{1,7},{2,4},{3,5},{4,2},{5,3},{6,0},{7,1},{8,14},{9,15},{10,... | collective-permute-start | bytes 602120 | tf_op jit(solution)/shard_map/ppermute | solution.py:458
  173.5 5.5 %collective-permute-start.34 = (bf16[17,16,128]{2,1,0:T(8,128)(2,1)S(1)}, bf16[17,16,128]{2,1,0:T(8,128)(2,1)S(1)}, u32[]{:S(2)}, u32[]{:S(2)}) collective-permute-start(bf16[17,16,128]{2,1,0:T(8,128)(2,1)S(1)} %get-tuple-element.175), channel_id=1, source_target_pairs={{0,8},{1,9},{2,10},{3,11},{4,12},{5,13},{6,14},{7,15},{8,0},{9,1},... | collective-permute-start | bytes 208904 | tf_op jit(solution)/shard_map/ppermute | solution.py:458
  174.0 6.7 %collective-permute-start.35 = (bf16[17,16,128]{2,1,0:T(8,128)(2,1)S(1)}, bf16[17,16,128]{2,1,0:T(8,128)(2,1)S(1)}, u32[]{:S(2)}, u32[]{:S(2)}) collective-permute-start(bf16[17,16,128]{2,1,0:T(8,128)(2,1)S(1)} %get-tuple-element.176), channel_id=1, source_target_pairs={{0,16},{1,17},{2,18},{3,19},{4,20},{5,21},{6,22},{7,23},{8,24},{9,... | collective-permute-start | bytes 208904 | tf_op jit(solution)/shard_map/ppermute | solution.py:458
  176.6 6.1 %collective-permute-start.36 = (bf16[17,16,128]{2,1,0:T(8,128)(2,1)S(1)}, bf16[17,16,128]{2,1,0:T(8,128)(2,1)S(1)}, u32[]{:S(2)}, u32[]{:S(2)}) collective-permute-start(bf16[17,16,128]{2,1,0:T(8,128)(2,1)S(1)} %get-tuple-element.177), channel_id=1, source_target_pairs={{0,24},{1,25},{2,26},{3,27},{4,28},{5,29},{6,30},{7,31},{8,16},{9,... | collective-permute-start | bytes 208904 | tf_op jit(solution)/shard_map/ppermute | solution.py:458
  (36 other events, 228.8 us)
